TPU v7x, 128 devices: a whole 4x4x4 slice. The times are simulated.
128 devices in a mesh: span: 8 (over y, core), chord: 16 (over z, x).
Axes of the slice: x: 4, y: 4, z: 4, core: 2. Of those that a mesh axis runs over, the one named last changes fastest.
Arguments:
- adjoint_source: float32 [6, 125, 32768], P(None, None, ('span', 'chord')), may hold values from -18 to 18
- degrees: int32 [32768], P(('span', 'chord')), may hold values from 1 to 4
- time_shift: float32 [32768], P(('span', 'chord')), may hold values from 1.5 to 4
- flux_jacobian: float32 [3, 6, 6, 32768], P(None, None, None, ('span', 'chord')), may hold values from -1.75 to 1.75
- block_inverse: float32 [6, 6, 32768], P(None, None, ('span', 'chord')), may hold values from -0.05 to 0.7, as said below
- dissipation: float32 [6, 6], replicated, may hold values from -0.45 to 0.7
- convection: float32 [6, 6], replicated, may hold values from -0.9 to 0.9
- face_weight: float32 [65536], P(('span', 'chord')), may hold values from 0.5 to 2
- face_elements: int32 [2, 65536], P(None, ('span', 'chord')), may hold values from 0 to 255
- face_numbers: int32 [2, 65536], P(None, ('span', 'chord')), may hold values from 0 to 5
- boundary_elements: int32 [4, 16384], P(None, ('span', 'chord')), may hold values from 0 to 255
- boundary_numbers: int32 [4, 16384], P(None, ('span', 'chord')), may hold values from 0 to 5
Outputs:
- adjoint: float32 [6, 125, 32768], P(None, None, ('span', 'chord'))
Inputs may be any that keep to these rules, and one draw needn't show every extreme that they name: `block_inverse`: diagonally dominant per element.
All inputs are finite; a program needn't handle non-finite values.
Results may differ from a plain program's by a relative error of at most 0.0024.
Values sent between devices are 32-bit elements; how exact they have to be, the bound alone decides.
A program may use at most 128 MiB of HBM per device.

v0:
```python
import jax
import jax.numpy as jnp
from jax import lax
from jax.sharding import PartitionSpec as P

ITERS = 4


HIGHEST = lax.Precision.HIGHEST


def extended(block, sides, width):
    for axis, dim in sides:
        count = lax.axis_size(axis)
        forward = [(i, i + 1) for i in range(count - 1)]
        backward = [(target, source) for source, target in forward]
        low = lax.ppermute(
            lax.slice_in_dim(block, block.shape[dim] - width, None, axis=dim), axis, forward
        )
        high = lax.ppermute(lax.slice_in_dim(block, 0, width, axis=dim), axis, backward)
        block = jnp.concatenate([low, block, high], axis=dim)
    return block


def tables():
    index = jnp.arange(5, dtype=jnp.int32)
    row_index = index[:, None]
    col_index = index[None, :]
    deriv = jnp.where(
        (col_index > row_index) & ((col_index - row_index) % 2 == 1),
        0.2 * (2 * row_index + 1).astype(jnp.float32),
        0.0,
    )
    alternate = jnp.where(index % 2 == 0, 1.0, -1.0).astype(jnp.float32)
    trace_table = 0.5 * jnp.stack([alternate, jnp.ones((5,), jnp.float32)])
    return (deriv, trace_table)


def active_modes(degrees):
    modes = jnp.arange(125, dtype=jnp.int32)
    highest = jnp.maximum(jnp.maximum(modes // 25, modes // 5 % 5), modes % 5)
    return (highest[:, None] <= degrees[None, :]).astype(jnp.float32)


def volume_term(field, time_shift, flux_jacobian, deriv):
    nvar, modes, count = field.shape
    cube = field.reshape(nvar, 5, 5, 5, count)
    result = time_shift[None, None, :] * field
    grads = [
        jnp.einsum("ji,bikle->bjkle", deriv, cube, precision=HIGHEST),
        jnp.einsum("ji,bkile->bkjle", deriv, cube, precision=HIGHEST),
        jnp.einsum("ji,bklie->bklje", deriv, cube, precision=HIGHEST),
    ]
    for direction in range(3):
        result = result + jnp.einsum(
            "abe,bme->ame",
            flux_jacobian[direction],
            grads[direction].reshape(nvar, modes, count),
            precision=HIGHEST,
        )
    return result


def face_traces(field, trace_table):
    nvar, modes, count = field.shape
    cube = field.reshape(nvar, 5, 5, 5, count)
    first = jnp.einsum("si,bijke->bjkse", trace_table, cube, precision=HIGHEST).reshape(
        nvar, 25, 2, count
    )
    second = jnp.einsum("sj,bijke->bikse", trace_table, cube, precision=HIGHEST).reshape(
        nvar, 25, 2, count
    )
    third = jnp.einsum("sk,bijke->bijse", trace_table, cube, precision=HIGHEST).reshape(
        nvar, 25, 2, count
    )
    return jnp.concatenate([first, second, third], axis=2)


def lift_faces(faces, trace_table):
    nvar = faces.shape[0]
    count = faces.shape[3]
    grid = faces.reshape(nvar, 5, 5, 6, count)
    result = jnp.einsum("si,bjkse->bijke", trace_table, grid[:, :, :, 0:2, :], precision=HIGHEST)
    result = result + jnp.einsum(
        "sj,bikse->bijke", trace_table, grid[:, :, :, 2:4, :], precision=HIGHEST
    )
    result = result + jnp.einsum(
        "sk,bijse->bijke", trace_table, grid[:, :, :, 4:6, :], precision=HIGHEST
    )
    return result.reshape(nvar, 125, count)


def face_flux(own_trace, other_trace, dissipation, convection, sign):
    nvar = dissipation.shape[0]
    difference = (own_trace - other_trace).reshape(nvar, 25, -1)
    combined = (own_trace + other_trace).reshape(nvar, 25, -1)
    result = jnp.einsum("xy,ymf->xmf", dissipation, difference, precision=HIGHEST)
    result = result + sign * jnp.einsum("xy,ymf->xmf", convection, combined, precision=HIGHEST)
    return result.reshape(own_trace.shape)


def span_terms(lower_side, upper_side, dissipation, convection):
    padded = extended(jnp.stack([lower_side, upper_side]), (("span", 0),), 1)
    return (
        face_flux(lower_side, padded[0], dissipation, convection, -1.0),
        face_flux(upper_side, padded[3], dissipation, convection, 1.0),
    )


def chord_terms(lower_side, upper_side, dissipation, convection):
    padded = extended(jnp.stack([lower_side, upper_side]), (("chord", 0),), 1)
    return (
        face_flux(lower_side, padded[0], dissipation, convection, -1.0),
        face_flux(upper_side, padded[3], dissipation, convection, 1.0),
    )


def squares(field):
    return lax.psum(jnp.sum(field * field), ("span", "chord"))


def local(
    adjoint_source,
    degrees,
    time_shift,
    flux_jacobian,
    block_inverse,
    dissipation,
    convection,
    face_weight,
    face_elements,
    face_numbers,
    boundary_elements,
    boundary_numbers,
):
    deriv, trace_table = tables()
    nvar, modes, count = adjoint_source.shape
    rows = nvar * 25
    active = active_modes(degrees)
    inner_cols = face_numbers * count + face_elements
    side_cols = boundary_numbers * count + boundary_elements
    source = active[None] * adjoint_source
    beta = jnp.sqrt(squares(source))
    basis = [source / beta]
    directions = []
    hess = jnp.zeros((ITERS + 1, ITERS), jnp.float32)
    for step in range(ITERS):
        direction = active[None] * jnp.einsum(
            "abe,bme->ame", block_inverse, basis[step], precision=HIGHEST
        )
        directions.append(direction)
        flat = face_traces(direction, trace_table).reshape(rows, 6 * count)
        left_trace = jnp.take(flat, inner_cols[0], axis=1)
        right_trace = jnp.take(flat, inner_cols[1], axis=1)
        term = (
            face_flux(left_trace, right_trace, dissipation, convection, 1.0) * face_weight[None, :]
        )
        gathered = (
            jnp.zeros_like(flat).at[:, inner_cols[0]].add(term).at[:, inner_cols[1]].add(-term)
        )
        sides = [jnp.take(flat, side_cols[side], axis=1) for side in range(4)]
        span_lower, span_upper = span_terms(sides[0], sides[1], dissipation, convection)
        chord_lower, chord_upper = chord_terms(sides[2], sides[3], dissipation, convection)
        gathered = gathered.at[:, side_cols[0]].add(span_lower).at[:, side_cols[1]].add(span_upper)
        gathered = (
            gathered.at[:, side_cols[2]].add(chord_lower).at[:, side_cols[3]].add(chord_upper)
        )
        result = volume_term(direction, time_shift, flux_jacobian, deriv) + lift_faces(
            gathered.reshape(nvar, 25, 6, count), trace_table
        )
        image = result * active[None]
        for position in range(step + 1):
            product = lax.psum(jnp.sum(basis[position] * image), ("span", "chord"))
            image = image - product * basis[position]
            hess = hess.at[position, step].set(product)
        length = jnp.sqrt(squares(image))
        hess = hess.at[step + 1, step].set(length)
        basis.append(image / length)
    normal = jnp.dot(hess.T, hess, precision=HIGHEST)
    factor = jnp.linalg.cholesky(normal)
    coeffs = jax.scipy.linalg.cho_solve((factor, True), beta * hess[0])
    adjoint = coeffs[0] * directions[0]
    for step in range(1, ITERS):
        adjoint = adjoint + coeffs[step] * directions[step]
    return adjoint


def solution(mesh):
    placed = (
        P(None, None, ("span", "chord")),
        P(("span", "chord")),
        P(("span", "chord")),
        P(None, None, None, ("span", "chord")),
        P(None, None, ("span", "chord")),
        P(),
        P(),
        P(("span", "chord")),
        P(None, ("span", "chord")),
        P(None, ("span", "chord")),
        P(None, ("span", "chord")),
        P(None, ("span", "chord")),
    )
    return jax.shard_map(
        local,
        mesh=mesh,
        in_specs=placed,
        out_specs=P(None, None, ("span", "chord")),
        check_vma=False,
    )
```

profile of v0, /device:TPU:1, one launch (start us, length us, event | category | flops | bytes accessed | tf_op | source)
XLA Modules:
  0.0 1564.2 jit_solution(13865155656635615881)
XLA Ops:
  2.6 68.7 %psum.105 = f32[]{:T(128)} all-reduce(f32[]{:T(128)} %multiply_reduce_fusion.14), channel_id=1, replica_groups=mesh['span'=8,'chord'=16] {'span','chord'}, use_global_device_ids=true, to_apply=%region_1.2 | all-reduce | flops 1 | bytes 8 | tf_op jit(solution)/shard_map/psum | solution.py:119
  147.2 4.2 scatter_fusion
  191.5 4.5 multiply_reduce_fusion.13
  196.0 66.9 %psum.106 = f32[]{:T(128)} all-reduce(f32[]{:T(128)} %get-tuple-element.266), channel_id=1, replica_groups=mesh['span'=8,'chord'=16] {'span','chord'}, use_global_device_ids=true, to_apply=%region_9.12 | all-reduce | flops 1 | bytes 8 | tf_op jit(solution)/shard_map/psum | solution.py:173
  265.0 64.3 %psum.107 = f32[]{:T(128)} all-reduce(f32[]{:T(128)} %multiply_reduce_fusion.12), channel_id=1, replica_groups=mesh['span'=8,'chord'=16] {'span','chord'}, use_global_device_ids=true, to_apply=%region_11.14 | all-reduce | flops 1 | bytes 8 | tf_op jit(solution)/shard_map/psum | solution.py:119
  404.8 5.2 scatter_custom_fusion.6
  413.2 6.1 scatter_fusion.5
  455.0 5.4 multiply_reduce_fusion.11
  460.4 67.0 %psum.108 = f32[]{:T(128)} all-reduce(f32[]{:T(128)} %get-tuple-element.268), channel_id=1, replica_groups=mesh['span'=8,'chord'=16] {'span','chord'}, use_global_device_ids=true, to_apply=%region_19.22 | all-reduce | flops 1 | bytes 8 | tf_op jit(solution)/shard_map/psum | solution.py:173
  530.8 64.1 %psum.109 = f32[]{:T(128)} all-reduce(f32[]{:T(128)} %multiply_reduce_fusion.10), channel_id=1, replica_groups=mesh['span'=8,'chord'=16] {'span','chord'}, use_global_device_ids=true, to_apply=%region_21.24 | all-reduce | flops 1 | bytes 8 | tf_op jit(solution)/shard_map/psum | solution.py:173
  599.0 62.7 %psum.110 = f32[]{:T(128)} all-reduce(f32[]{:T(128)} %get-tuple-element.181), channel_id=1, replica_groups=mesh['span'=8,'chord'=16] {'span','chord'}, use_global_device_ids=true, to_apply=%region_23.26 | all-reduce | flops 1 | bytes 8 | tf_op jit(solution)/shard_map/psum | solution.py:119
  738.4 5.1 scatter_custom_fusion.12
  749.8 6.2 scatter_fusion.10
  792.0 5.5 multiply_reduce_fusion.8
  797.5 66.7 %psum.111 = f32[]{:T(128)} all-reduce(f32[]{:T(128)} %get-tuple-element.270), channel_id=1, replica_groups=mesh['span'=8,'chord'=16] {'span','chord'}, use_global_device_ids=true, to_apply=%region_32.35 | all-reduce | flops 1 | bytes 8 | tf_op jit(solution)/shard_map/psum | solution.py:173
  867.8 63.0 %psum.112 = f32[]{:T(128)} all-reduce(f32[]{:T(128)} %multiply_reduce_fusion.7), channel_id=1, replica_groups=mesh['span'=8,'chord'=16] {'span','chord'}, use_global_device_ids=true, to_apply=%region_34.37 | all-reduce | flops 1 | bytes 8 | tf_op jit(solution)/shard_map/psum | solution.py:173
  930.9 5.2 multiply_reduce_fusion.6
  936.0 63.8 %psum.113 = f32[]{:T(128)} all-reduce(f32[]{:T(128)} %get-tuple-element.179), channel_id=1, replica_groups=mesh['span'=8,'chord'=16] {'span','chord'}, use_global_device_ids=true, to_apply=%region_36.39 | all-reduce | flops 1 | bytes 8 | tf_op jit(solution)/shard_map/psum | solution.py:173
  1004.4 63.1 %psum.114 = f32[]{:T(128)} all-reduce(f32[]{:T(128)} %multiply_reduce_fusion.5), channel_id=1, replica_groups=mesh['span'=8,'chord'=16] {'span','chord'}, use_global_device_ids=true, to_apply=%region_38.41 | all-reduce | flops 1 | bytes 8 | tf_op jit(solution)/shard_map/psum | solution.py:119
  1068.1 5.2 fusion.12
  1151.2 5.1 scatter_custom_fusion.18
  1161.3 6.2 scatter_fusion.15
  1186.7 4.2 scatter_fusion.19
  1203.7 5.5 multiply_reduce_fusion.4
  1209.2 66.8 %psum.115 = f32[]{:T(128)} all-reduce(f32[]{:T(128)} %get-tuple-element.272), channel_id=1, replica_groups=mesh['span'=8,'chord'=16] {'span','chord'}, use_global_device_ids=true, to_apply=%region_47.50 | all-reduce | flops 1 | bytes 8 | tf_op jit(solution)/shard_map/psum | solution.py:173
  1279.6 62.8 %psum.116 = f32[]{:T(128)} all-reduce(f32[]{:T(128)} %multiply_reduce_fusion.3), channel_id=1, replica_groups=mesh['span'=8,'chord'=16] {'span','chord'}, use_global_device_ids=true, to_apply=%region_49.52 | all-reduce | flops 1 | bytes 8 | tf_op jit(solution)/shard_map/psum | solution.py:173
  1342.4 5.2 multiply_reduce_fusion.2
  1347.6 63.9 %psum.117 = f32[]{:T(128)} all-reduce(f32[]{:T(128)} %get-tuple-element.177), channel_id=1, replica_groups=mesh['span'=8,'chord'=16] {'span','chord'}, use_global_device_ids=true, to_apply=%region_51.54 | all-reduce | flops 1 | bytes 8 | tf_op jit(solution)/shard_map/psum | solution.py:173
  1417.3 62.6 %psum.118 = f32[]{:T(128)} all-reduce(f32[]{:T(128)} %multiply_reduce_fusion.1), channel_id=1, replica_groups=mesh['span'=8,'chord'=16] {'span','chord'}, use_global_device_ids=true, to_apply=%region_53.56 | all-reduce | flops 1 | bytes 8 | tf_op jit(solution)/shard_map/psum | solution.py:173
  1479.8 4.4 multiply_reduce_fusion
  1487.4 64.3 %psum.119 = f32[]{:T(128)} all-reduce(f32[]{:T(128)} %multiply_reduce_fusion), channel_id=1, replica_groups=mesh['span'=8,'chord'=16] {'span','chord'}, use_global_device_ids=true, to_apply=%region_55.58 | all-reduce | flops 1 | bytes 8 | tf_op jit(solution)/shard_map/psum | solution.py:119
  1558.1 4.7 multiply_add_fusion
  (739 shorter events, 495.1 us)
Async XLA Ops:
  0.0 126.6 %copy-start = (f32[6,6]{1,0:T(8,128)S(1)}, f32[6,6]{1,0:T(8,128)}, u32[]{:S(2)}) copy-start(f32[6,6]{1,0:T(8,128)} %param.49) | copy-start | bytes 436
  0.0 72.0 %copy-start.60 = (f32[6,6,256]{2,1,0:T(8,128)S(1)}, f32[6,6,256]{2,1,0:T(8,128)}, u32[]{:S(2)}) copy-start(f32[6,6,256]{2,1,0:T(8,128)} %param.48) | copy-start | bytes 110596
  81.5 20.4 %copy-start.69 = (pred[128]{0:T(512)(128)(4,1)}, pred[128]{0:T(512)(128)(4,1)S(1)}, u32[]{:S(2)}) copy-start(pred[128]{0:T(512)(128)(4,1)S(1)} %get-tuple-element.250) | copy-start | bytes 388
  86.2 15.6 copy-start.38
  87.0 71.9 %collective-permute-start.2 = (f32[1,150,128]{1,2,0:T(8,128)}, f32[1,150,128]{1,2,0:T(8,128)}, u32[]{:S(2)}, u32[]{:S(2)}) collective-permute-start(f32[1,150,128]{1,2,0:T(8,128)} %select_bitcast_fusion.12), channel_id=1, source_target_pairs={{0,1},{1,2},{2,3},{3,4},{4,5},{5,6},{6,7},{7,8},{8,9},{9,10},{10,1... | collective-permute-start | bytes 230408 | tf_op jit(solution)/shard_map/ppermute | solution.py:17
  91.8 17.7 %copy-start.40 = (f32[128,150]{1,0:T(8,128)}, f32[128,150]{1,0:T(8,128)S(1)}, u32[]{:S(2)}) copy-start(f32[128,150]{1,0:T(8,128)S(1)} %gather_fusion.4) | copy-start | bytes 230404
  92.6 69.8 %collective-permute-start.3 = (f32[1,150,128]{1,2,0:T(8,128)}, f32[1,150,128]{1,2,0:T(8,128)}, u32[]{:S(2)}, u32[]{:S(2)}) collective-permute-start(f32[1,150,128]{1,2,0:T(8,128)} %select_bitcast_fusion.13), channel_id=1, source_target_pairs={{1,0},{2,1},{3,2},{4,3},{5,4},{6,5},{7,6},{8,7},{9,8},{10,9},{11,1... | collective-permute-start | bytes 230408 | tf_op jit(solution)/shard_map/ppermute | solution.py:20
  93.9 15.6 copy-start.125
  96.8 69.3 %collective-permute-start = (f32[1,150,128]{1,2,0:T(8,128)}, f32[1,150,128]{1,2,0:T(8,128)}, u32[]{:S(2)}, u32[]{:S(2)}) collective-permute-start(f32[1,150,128]{1,2,0:T(8,128)} %select_bitcast_fusion.14), channel_id=1, source_target_pairs={{0,16},{16,32},{32,48},{48,64},{64,80},{80,96},{96,112},{1,17},{17... | collective-permute-start | bytes 230408 | tf_op jit(solution)/shard_map/ppermute | solution.py:17
  102.6 68.7 %collective-permute-start.1 = (f32[1,150,128]{1,2,0:T(8,128)}, f32[1,150,128]{1,2,0:T(8,128)}, u32[]{:S(2)}, u32[]{:S(2)}) collective-permute-start(f32[1,150,128]{1,2,0:T(8,128)} %select_bitcast_fusion.15), channel_id=1, source_target_pairs={{16,0},{32,16},{48,32},{64,48},{80,64},{96,80},{112,96},{17,1},{33... | collective-permute-start | bytes 230408 | tf_op jit(solution)/shard_map/ppermute | solution.py:20
  105.1 261.7 %copy-start.54 = (f32[5]{0:T(128)}, f32[5]{0:T(128)S(1)}, u32[]{:S(2)}) copy-start(f32[5]{0:T(128)S(1)} %convert_multiply_fusion) | copy-start | bytes 64
  196.0 68.4 %copy-start.131 = (s32[2]{0:T(128)S(1)}, s32[2]{0:T(128)}, u32[]{:S(2)}) copy-start(s32[2]{0:T(128)} %iota_multiply_fusion.1) | copy-start | bytes 28
  196.0 134.0 %copy-start.37 = (f32[6,6,256]{1,0,2:T(8,128)S(1)}, f32[6,6,256]{1,0,2:T(8,128)}, u32[]{:S(2)}) copy-start(f32[6,6,256]{1,0,2:T(8,128)} %copy.113) | copy-start | bytes 110596
  372.9 46.4 %collective-permute-start.6 = (f32[1,150,128]{1,2,0:T(8,128)}, f32[1,150,128]{1,2,0:T(8,128)}, u32[]{:S(2)}, u32[]{:S(2)}) collective-permute-start(f32[1,150,128]{1,2,0:T(8,128)} %select_bitcast_fusion.8), channel_id=1, source_target_pairs={{0,1},{1,2},{2,3},{3,4},{4,5},{5,6},{6,7},{7,8},{8,9},{9,10},{10,1... | collective-permute-start | bytes 230408 | tf_op jit(solution)/shard_map/ppermute | solution.py:17
  374.8 45.8 %collective-permute-start.7 = (f32[1,150,128]{1,2,0:T(8,128)}, f32[1,150,128]{1,2,0:T(8,128)}, u32[]{:S(2)}, u32[]{:S(2)}) collective-permute-start(f32[1,150,128]{1,2,0:T(8,128)} %select_bitcast_fusion.9), channel_id=1, source_target_pairs={{1,0},{2,1},{3,2},{4,3},{5,4},{6,5},{7,6},{8,7},{9,8},{10,9},{11,1... | collective-permute-start | bytes 230408 | tf_op jit(solution)/shard_map/ppermute | solution.py:20
  376.1 46.2 %collective-permute-start.4 = (f32[1,150,128]{1,2,0:T(8,128)}, f32[1,150,128]{1,2,0:T(8,128)}, u32[]{:S(2)}, u32[]{:S(2)}) collective-permute-start(f32[1,150,128]{1,2,0:T(8,128)} %select_bitcast_fusion.10), channel_id=1, source_target_pairs={{0,16},{16,32},{32,48},{48,64},{64,80},{80,96},{96,112},{1,17},{17... | collective-permute-start | bytes 230408 | tf_op jit(solution)/shard_map/ppermute | solution.py:17
  379.7 45.4 %collective-permute-start.5 = (f32[1,150,128]{1,2,0:T(8,128)}, f32[1,150,128]{1,2,0:T(8,128)}, u32[]{:S(2)}, u32[]{:S(2)}) collective-permute-start(f32[1,150,128]{1,2,0:T(8,128)} %select_bitcast_fusion.11), channel_id=1, source_target_pairs={{16,0},{32,16},{48,32},{64,48},{80,64},{96,80},{112,96},{17,1},{33... | collective-permute-start | bytes 230408 | tf_op jit(solution)/shard_map/ppermute | solution.py:20
  599.0 63.4 %copy-start.2 = (f32[6,125,256]{1,0,2:T(8,128)}, f32[6,125,256]{1,0,2:T(8,128)S(1)}, u32[]{:S(2)}) copy-start(f32[6,125,256]{1,0,2:T(8,128)S(1)} %get-tuple-element.182) | copy-start | bytes 2304004
  699.7 15.4 copy-start.32
  699.7 15.4 copy-start.33
  705.2 50.7 %collective-permute-start.10 = (f32[1,150,128]{1,2,0:T(8,128)}, f32[1,150,128]{1,2,0:T(8,128)}, u32[]{:S(2)}, u32[]{:S(2)}) collective-permute-start(f32[1,150,128]{1,2,0:T(8,128)} %select_bitcast_fusion.4), channel_id=1, source_target_pairs={{0,1},{1,2},{2,3},{3,4},{4,5},{5,6},{6,7},{7,8},{8,9},{9,10},{10,1... | collective-permute-start | bytes 230408 | tf_op jit(solution)/shard_map/ppermute | solution.py:17
  708.7 48.7 %collective-permute-start.11 = (f32[1,150,128]{1,2,0:T(8,128)}, f32[1,150,128]{1,2,0:T(8,128)}, u32[]{:S(2)}, u32[]{:S(2)}) collective-permute-start(f32[1,150,128]{1,2,0:T(8,128)} %select_bitcast_fusion.5), channel_id=1, source_target_pairs={{1,0},{2,1},{3,2},{4,3},{5,4},{6,5},{7,6},{8,7},{9,8},{10,9},{11,1... | collective-permute-start | bytes 230408 | tf_op jit(solution)/shard_map/ppermute | solution.py:20
  710.0 49.0 %collective-permute-start.8 = (f32[1,150,128]{1,2,0:T(8,128)}, f32[1,150,128]{1,2,0:T(8,128)}, u32[]{:S(2)}, u32[]{:S(2)}) collective-permute-start(f32[1,150,128]{1,2,0:T(8,128)} %select_bitcast_fusion.6), channel_id=1, source_target_pairs={{0,16},{16,32},{32,48},{48,64},{64,80},{80,96},{96,112},{1,17},{17... | collective-permute-start | bytes 230408 | tf_op jit(solution)/shard_map/ppermute | solution.py:17
  712.0 49.8 %collective-permute-start.9 = (f32[1,150,128]{1,2,0:T(8,128)}, f32[1,150,128]{1,2,0:T(8,128)}, u32[]{:S(2)}, u32[]{:S(2)}) collective-permute-start(f32[1,150,128]{1,2,0:T(8,128)} %select_bitcast_fusion.7), channel_id=1, source_target_pairs={{16,0},{32,16},{48,32},{64,48},{80,64},{96,80},{112,96},{17,1},{33... | collective-permute-start | bytes 230408 | tf_op jit(solution)/shard_map/ppermute | solution.py:20
  864.2 66.7 %copy-start.3 = (f32[6,125,256]{1,0,2:T(8,128)S(1)}, f32[6,125,256]{1,0,2:T(8,128)}, u32[]{:S(2)}) copy-start(f32[6,125,256]{1,0,2:T(8,128)} %copy-done.2) | copy-start | bytes 2304004
  1117.0 50.5 %collective-permute-start.14 = (f32[1,150,128]{1,2,0:T(8,128)}, f32[1,150,128]{1,2,0:T(8,128)}, u32[]{:S(2)}, u32[]{:S(2)}) collective-permute-start(f32[1,150,128]{1,2,0:T(8,128)} %select_bitcast_fusion), channel_id=1, source_target_pairs={{0,1},{1,2},{2,3},{3,4},{4,5},{5,6},{6,7},{7,8},{8,9},{9,10},{10,1... | collective-permute-start | bytes 230408 | tf_op jit(solution)/shard_map/ppermute | solution.py:17
  1120.4 48.5 %collective-permute-start.15 = (f32[1,150,128]{1,2,0:T(8,128)}, f32[1,150,128]{1,2,0:T(8,128)}, u32[]{:S(2)}, u32[]{:S(2)}) collective-permute-start(f32[1,150,128]{1,2,0:T(8,128)} %select_bitcast_fusion.1), channel_id=1, source_target_pairs={{1,0},{2,1},{3,2},{4,3},{5,4},{6,5},{7,6},{8,7},{9,8},{10,9},{11,1... | collective-permute-start | bytes 230408 | tf_op jit(solution)/shard_map/ppermute | solution.py:20
  1121.7 48.9 %collective-permute-start.12 = (f32[1,150,128]{1,2,0:T(8,128)}, f32[1,150,128]{1,2,0:T(8,128)}, u32[]{:S(2)}, u32[]{:S(2)}) collective-permute-start(f32[1,150,128]{1,2,0:T(8,128)} %select_bitcast_fusion.2), channel_id=1, source_target_pairs={{0,16},{16,32},{32,48},{48,64},{64,80},{80,96},{96,112},{1,17},{17... | collective-permute-start | bytes 230408 | tf_op jit(solution)/shard_map/ppermute | solution.py:17
  1123.7 49.7 %collective-permute-start.13 = (f32[1,150,128]{1,2,0:T(8,128)}, f32[1,150,128]{1,2,0:T(8,128)}, u32[]{:S(2)}, u32[]{:S(2)}) collective-permute-start(f32[1,150,128]{1,2,0:T(8,128)} %select_bitcast_fusion.3), channel_id=1, source_target_pairs={{16,0},{32,16},{48,32},{64,48},{80,64},{96,80},{112,96},{17,1},{33... | collective-permute-start | bytes 230408 | tf_op jit(solution)/shard_map/ppermute | solution.py:20
  1275.9 66.4 %copy-start.4 = (f32[6,125,256]{1,0,2:T(8,128)S(1)}, f32[6,125,256]{1,0,2:T(8,128)}, u32[]{:S(2)}) copy-start(f32[6,125,256]{1,0,2:T(8,128)} %copy-done.2) | copy-start | bytes 2304004
  1411.5 68.3 %copy-start.19 = (f32[6,125,256]{1,0,2:T(8,128)S(1)}, f32[6,125,256]{1,0,2:T(8,128)}, u32[]{:S(2)}) copy-start(f32[6,125,256]{1,0,2:T(8,128)} %get-tuple-element.180) | copy-start | bytes 2304004
  1479.8 78.2 %copy-start.21 = (f32[6,125,256]{1,0,2:T(8,128)S(1)}, f32[6,125,256]{1,0,2:T(8,128)}, u32[]{:S(2)}) copy-start(f32[6,125,256]{1,0,2:T(8,128)} %copy-done.20) | copy-start | bytes 2304004
  (118 other events, 604.7 us)
where the time goes:
time: 1580 us; the launch traced here: 1560 us
  blocking collectives  971 us (61%)
  local copies, waits for them, and re-layouts  218 us (14%)
  other arithmetic  180 us (11%)
  matrix products  147 us (9%)
  starting transfers between devices  37.7 us (2%)
    psum x10, blocking collectives, local(): product = lax.psum(jnp.sum(basis[position] * image), ('span', 'chord'))  648 us
    psum x5, blocking collectives, squares(): return lax.psum(jnp.sum(field * field), ('span', 'chord'))  323 us
    dot_general x12, matrix products, volume_term(): jnp.einsum('abe,bme->ame', flux_jacobian[direction], grads[direction].res...  46.7 us
    scatter-add x8, other arithmetic, local(): jnp.zeros_like(flat).at[:, inner_cols[0]].add(term).at[:, inner_cols[1]]  42.2 us
    gather x16, local copies, waits for them, and re-layouts, local(): sides = [jnp.take(flat, side_cols[side], axis=1) for side in range(4)]  40 us
  transfers between devices with their start and end apart: 16, of which 0 were waited for; matrix products, arithmetic and copies ran while one was open for 13% of the time, Pallas kernels for 0%

commit v1 on v0

v1 whole, which is shorter than its diff:
```python
import functools

import jax
import jax.numpy as jnp
import numpy as np
from jax import lax
from jax.experimental import pallas as pl
from jax.experimental.pallas import tpu as pltpu
from jax.sharding import PartitionSpec as P

ITERS = 4
NV = 6
E = 256
IF = 512
FS = 128
NF = 6
ROWS = 160
SEND = 152
COLS = NF * E
SLOTS = 2 * IF + 4 * FS
SHIFT = 1.5
MESH = pl.DeviceIdType.MESH
BF = jnp.bfloat16
F32 = jnp.float32


def face_row(face, t):
    return face * 24 + t if t < 24 else 144 + face


def constants():
    mode_mat = np.zeros((ROWS + 384, 128), np.float32)
    lift = np.zeros((128, ROWS), np.float32)
    sign = [1.0, -1.0, 1.0, -1.0, 1.0]
    for i in range(5):
        for j in range(5):
            for k in range(5):
                m = 25 * i + 5 * j + k
                idx = (i, j, k)
                rest = (5 * j + k, 5 * i + k, 5 * i + j)
                step = (25, 5, 1)
                for d in range(3):
                    for end in range(2):
                        r = face_row(2 * d + end, rest[d])
                        value = 0.5 * (sign[idx[d]] if end == 0 else 1.0)
                        mode_mat[r, m] = value
                        lift[m, r] = value
                    for low in range(idx[d]):
                        if (idx[d] - low) % 2 == 1:
                            out = m - step[d] * (idx[d] - low)
                            mode_mat[ROWS + 128 * d + out, m] = 2 * low + 1
    highest = np.full((128, 128), 99, np.int32)
    for m in range(125):
        highest[m] = max(m // 25, m // 5 % 5, m % 5)
    return (
        jnp.asarray(np.concatenate([mode_mat, mode_mat], axis=1), BF),
        jnp.asarray(np.concatenate([lift, lift], axis=1), BF),
        jnp.asarray(highest),
    )


def split(x):
    hi = x.astype(BF)
    return hi, (x - hi.astype(F32)).astype(BF)


def dot(a, b):
    return jnp.dot(a, b, preferred_element_type=F32)


def dot_t(a, b):
    return lax.dot_general(a, b, (((1,), (1,)), ((), ())), preferred_element_type=F32)


def kernel(
    n_span,
    n_chord,
    src,
    degrees,
    time_shift,
    jac,
    binv,
    diss,
    conv,
    weight,
    face_el,
    face_no,
    side_el,
    side_no,
    mode_mat,
    lift_mat,
    highest,
    out,
    active,
    jac2,
    select,
    mix,
    us,
    zs,
    modes,
    grads,
    flat,
    flat_b,
    own,
    interior,
    uv_b,
    term_b,
    gathered,
    faces,
    sends,
    recvs,
    gram,
    red1,
    red2,
    send_sem,
    recv_sem,
    r1_send,
    r1_recv,
    r2_send,
    r2_recv,
):
    span = lax.axis_index("span")
    chord = lax.axis_index("chord")

    barrier = pltpu.get_barrier_semaphore()
    for i in range(1, n_span):
        pl.semaphore_signal(
            barrier, inc=1, device_id=(lax.rem(span + i, n_span), chord), device_id_type=MESH
        )
    for i in range(1, n_chord):
        pl.semaphore_signal(
            barrier, inc=1, device_id=(span, lax.rem(chord + i, n_chord)), device_id_type=MESH
        )

    has = (span > 0, span < n_span - 1, chord > 0, chord < n_chord - 1)
    targets = ((span - 1, chord), (span + 1, chord), (span, chord - 1), (span, chord + 1))

    act = (highest[:, 0:1] <= degrees[...].reshape(1, E)).astype(F32)
    active[...] = act
    for b in range(NV):
        us[0, b, 125:128, :] = jnp.zeros((3, E), F32)
        us[0, b, 0:125, :] = src[b] * act[0:125]
    jac2[...] = jac[...] * 0.2

    cols_in = face_no[...] * E + face_el[...]
    cols_sd = side_no[...] * E + side_el[...]
    left = cols_in[0:1, :]
    right = cols_in[1:2, :]
    row16 = lax.broadcasted_iota(jnp.int32, (16, FS), 0)

    def build(c, carry):
        base = pl.multiple_of(c * 16, 16)
        rows = row16 + base
        for q in range(4):
            l = (rows == left[:, q * FS : (q + 1) * FS]).astype(F32)
            r = (rows == right[:, q * FS : (q + 1) * FS]).astype(F32)
            s = (rows == cols_sd[q : q + 1, :]).astype(F32)
            select[pl.ds(base, 16), q * FS : (q + 1) * FS] = (l - r).astype(BF)
            select[pl.ds(base, 16), IF + q * FS : IF + (q + 1) * FS] = (l + r).astype(BF)
            select[pl.ds(base, 16), 2 * IF + q * FS : 2 * IF + (q + 1) * FS] = s.astype(BF)
        return carry

    lax.fori_loop(0, COLS // 16, build, 0)

    r24 = lax.broadcasted_iota(jnp.int32, (24, ROWS), 0)
    c24 = lax.broadcasted_iota(jnp.int32, (24, ROWS), 1)
    r16 = lax.broadcasted_iota(jnp.int32, (16, ROWS), 0)
    c16 = lax.broadcasted_iota(jnp.int32, (16, ROWS), 1)
    mixed = []
    for mat in (diss, conv):
        parts = []
        for x in range(NV):
            acc = jnp.zeros((24, ROWS), F32)
            for y in range(NV):
                acc = acc + jnp.where(c24 == r24 + y * 24, mat[x, y], 0.0)
            parts.append(acc)
        acc = jnp.zeros((16, ROWS), F32)
        for x in range(NV):
            for y in range(NV):
                acc = acc + jnp.where((r16 == x) & (c16 == 144 + y), mat[x, y], 0.0)
        parts.append(acc)
        mixed.append(jnp.concatenate(parts, axis=0))
    mixed = jnp.concatenate(mixed, axis=1)
    mix_hi, mix_lo = split(mixed)
    mix[:, 0 : 2 * ROWS] = mix_hi
    mix[:, 2 * ROWS : 4 * ROWS] = mix_hi
    mix[:, 4 * ROWS : 6 * ROWS] = mix_lo

    flat[...] = jnp.zeros_like(flat)
    faces[...] = jnp.zeros_like(faces)
    for s in range(4):

        @pl.when(jnp.logical_not(has[s]))
        def _(s=s):
            for k in range(ITERS):
                recvs[k, s] = jnp.zeros((SEND, FS), F32)

    pl.semaphore_wait(barrier, n_span + n_chord - 2)

    def side_copy(step, s):
        return pltpu.make_async_remote_copy(
            src_ref=sends.at[step, s],
            dst_ref=recvs.at[step, s ^ 1],
            send_sem=send_sem.at[step, s],
            recv_sem=recv_sem.at[step, s ^ 1],
            device_id=targets[s],
            device_id_type=MESH,
        )

    def mix_terms(difference, total):
        d_hi, d_lo = split(difference)
        t_hi, t_lo = split(total)
        n = difference.shape[1]
        for k, part in enumerate((d_hi, t_hi, d_lo, t_lo, d_hi, t_hi)):
            uv_b[k * ROWS : (k + 1) * ROWS, 0:n] = part
        return dot(mix[...], uv_b[:, 0:n])

    def one_step(step, carry):
        for lt in range(2):
            lanes = slice(lt * 128, (lt + 1) * 128)
            for a0 in range(0, NV, 2):
                acc = [None, None]
                for b in range(NV):
                    u = us[step, b, :, lanes]
                    for p in range(2):
                        t = binv[a0 + p, b : b + 1, lanes] * u
                        acc[p] = t if acc[p] is None else acc[p] + t
                for p in range(2):
                    zs[step, a0 + p, :, lanes] = acc[p]
                    hi, lo = split(acc[p])
                    modes[a0 + p, 0:128, lanes] = hi
                    modes[a0 + p, 128:256, lanes] = lo
        for b in range(NV):
            t = dot(mode_mat[0:ROWS, :], modes[b])
            for f in range(NF):
                flat[b * 24 : (b + 1) * 24, f * E : (f + 1) * E] = t[f * 24 : (f + 1) * 24]
                flat[144 + b : 145 + b, f * E : (f + 1) * E] = t[144 + f : 145 + f]
        for f in range(NF):
            hi, lo = split(flat[:, f * E : (f + 1) * E])
            flat_b[0:ROWS, f * E : (f + 1) * E] = hi
            flat_b[ROWS : 2 * ROWS, f * E : (f + 1) * E] = lo
        t = dot(flat_b[...], select[:, 2 * IF :])
        own[...] = t[0:ROWS] + t[ROWS:]
        for s in range(4):
            sends[step, s] = own[0:SEND, s * FS : (s + 1) * FS]

            @pl.when(has[s])
            def _(s=s):
                side_copy(step, s).start()

        for b in range(NV):
            grads[b] = dot(mode_mat[ROWS:, :], modes[b])
        for q in range(2):
            t = dot(flat_b[...], select[:, q * IF : (q + 1) * IF])
            interior[q] = t[0:ROWS] + t[ROWS:]
        term = mix_terms(interior[0], interior[1]) * weight[...].reshape(1, IF)
        hi, lo = split(term)
        term_b[0:ROWS] = hi
        term_b[ROWS:] = lo
        for f in range(NF):
            t = dot_t(term_b[...], select[f * E : (f + 1) * E, 0:IF])
            gathered[:, f * E : (f + 1) * E] = t[0:ROWS] + t[ROWS:]
        for lt in range(2):
            lanes = slice(lt * 128, (lt + 1) * 128)
            shift = time_shift[...].reshape(1, E)[:, lanes]
            for a0 in range(0, NV, 2):
                acc = [shift * zs[step, a0 + p, :, lanes] for p in range(2)]
                for d in range(3):
                    for b in range(NV):
                        g = grads[b, d * 128 : (d + 1) * 128, lanes]
                        for p in range(2):
                            acc[p] = acc[p] + jac2[d, a0 + p, b : b + 1, lanes] * g
                for p in range(2):
                    us[step + 1, a0 + p, :, lanes] = acc[p]
        for s in range(4):

            @pl.when(has[s])
            def _(s=s):
                side_copy(step, s ^ 1).wait_recv()

        diffs, sums = [], []
        for s in range(4):
            mine = own[:, s * FS : (s + 1) * FS]
            other = jnp.concatenate([recvs[step, s], jnp.zeros((ROWS - SEND, FS), F32)], axis=0)
            diffs.append(mine - other)
            sums.append(mine + other if s % 2 == 1 else -(mine + other))
        term = mix_terms(jnp.concatenate(diffs, axis=1), jnp.concatenate(sums, axis=1))
        hi, lo = split(term)
        term_b[0:ROWS] = hi
        term_b[ROWS:] = lo
        for f in range(NF):
            t = dot_t(term_b[...], select[f * E : (f + 1) * E, 2 * IF :])
            t = gathered[:, f * E : (f + 1) * E] + (t[0:ROWS] + t[ROWS:])
            for b in range(NV):
                faces[b, f * 24 : (f + 1) * 24, :] = t[b * 24 : (b + 1) * 24]
                faces[b, 144 + f : 145 + f, :] = t[144 + b : 145 + b]
        for b in range(NV):
            hi, lo = split(faces[b])
            t = dot(lift_mat[...], jnp.concatenate([hi, lo], axis=0))
            us[step + 1, b] = (us[step + 1, b] + t) * active[...] - SHIFT * us[step, b]
        for s in range(4):

            @pl.when(has[s])
            def _(s=s):
                side_copy(step, s).wait_send()

        return carry

    lax.fori_loop(0, ITERS, one_step, 0)

    pairs = [(i, j) for i in range(ITERS + 1) for j in range(i, ITERS + 1)]

    def products(c, accs):
        accs = list(accs)
        base = pl.multiple_of(c * 8, 8)
        for b in range(NV):
            for lt in range(2):
                lanes = slice(lt * 128, (lt + 1) * 128)
                u = [us[k, b, pl.ds(base, 8), lanes] for k in range(ITERS + 1)]
                for n, (i, j) in enumerate(pairs):
                    accs[n] = accs[n] + u[i] * u[j]
        return tuple(accs)

    accs = lax.fori_loop(0, 16, products, tuple(jnp.zeros((8, 128), F32) for _ in pairs))
    rows = [jnp.sum(x, axis=0, keepdims=True) for x in accs]
    rows.append(jnp.zeros((1, 128), F32))
    x = jnp.concatenate(rows, axis=0)
    for amount in (64, 32, 16, 8):
        x = x + pltpu.roll(x, amount, 1)
    row = lax.broadcasted_iota(jnp.int32, (16, 128), 0)
    lane = lax.broadcasted_iota(jnp.int32, (16, 128), 1)
    x = jnp.sum(jnp.where((lane >= row * 8) & (lane < row * 8 + 8), x, 0.0), axis=0, keepdims=True)
    gram[0] = jnp.broadcast_to(x, (8, 128))

    def r1_copy(i):
        return pltpu.make_async_remote_copy(
            src_ref=gram.at[0],
            dst_ref=red1.at[i],
            send_sem=r1_send.at[i],
            recv_sem=r1_recv.at[i],
            device_id=(lax.rem(span + i, n_span), chord),
            device_id_type=MESH,
        )

    def r2_copy(i):
        return pltpu.make_async_remote_copy(
            src_ref=gram.at[1],
            dst_ref=red2.at[i],
            send_sem=r2_send.at[i],
            recv_sem=r2_recv.at[i],
            device_id=(span, lax.rem(chord + i, n_chord)),
            device_id_type=MESH,
        )

    for i in range(1, n_span):
        r1_copy(i).start()
    total = gram[0]
    for i in range(1, n_span):
        r1_copy(i).wait_recv()
        total = total + red1[i]
    gram[1] = total
    for i in range(1, n_chord):
        r2_copy(i).start()
    total = gram[1]
    for i in range(1, n_chord):
        r2_copy(i).wait_recv()
        total = total + red2[i]
    for amount in (4, 2, 1):
        total = total + pltpu.roll(total, 128 - amount, 1)

    g = {}
    for n, (i, j) in enumerate(pairs):
        g[i, j] = g[j, i] = jnp.broadcast_to(total[:, 8 * n : 8 * n + 1], (8, 128))
    half = [[SHIFT * g[i, j] + g[i, j + 1] for j in range(ITERS)] for i in range(ITERS + 1)]
    normal = [
        [SHIFT * half[i][j] + half[i + 1][j] for j in range(ITERS)] for i in range(ITERS)
    ]
    rhs = [half[0][j] for j in range(ITERS)]
    low = [[None] * ITERS for _ in range(ITERS)]
    pivot, inv = [], []
    for j in range(ITERS):
        d = normal[j][j]
        for k in range(j):
            d = d - low[j][k] * low[j][k] * pivot[k]
        pivot.append(d)
        usable = d > 1e-6 * normal[j][j]
        inv.append(jnp.where(usable, 1.0 / jnp.where(usable, d, 1.0), 0.0))
        for i in range(j + 1, ITERS):
            v = normal[i][j]
            for k in range(j):
                v = v - low[i][k] * low[j][k] * pivot[k]
            low[i][j] = v * inv[j]
    y = []
    for i in range(ITERS):
        v = rhs[i]
        for k in range(i):
            v = v - low[i][k] * y[k]
        y.append(v)
    coeffs = [y[i] * inv[i] for i in range(ITERS)]
    for i in reversed(range(ITERS)):
        for k in range(i + 1, ITERS):
            coeffs[i] = coeffs[i] - low[k][i] * coeffs[k]
    coeffs = [c[0:1, :] for c in coeffs]
    for b in range(NV):
        for lt in range(2):
            lanes = slice(lt * 128, (lt + 1) * 128)
            x = coeffs[0] * zs[0, b, 0:125, lanes]
            for k in range(1, ITERS):
                x = x + coeffs[k] * zs[k, b, 0:125, lanes]
            out[b, :, lanes] = x

    for i in range(1, n_span):
        r1_copy(i).wait_send()
    for i in range(1, n_chord):
        r2_copy(i).wait_send()


def local(n_span, n_chord, *args):
    vmem = pl.BlockSpec(memory_space=pltpu.VMEM)
    smem = pl.BlockSpec(memory_space=pltpu.SMEM)
    specs = [vmem] * 15
    specs[5] = specs[6] = smem
    return pl.pallas_call(
        functools.partial(kernel, n_span, n_chord),
        out_shape=jax.ShapeDtypeStruct((NV, 125, E), F32),
        in_specs=specs,
        out_specs=vmem,
        scratch_shapes=[
            pltpu.VMEM((128, E), F32),
            pltpu.VMEM((3, NV, NV, E), F32),
            pltpu.VMEM((COLS, SLOTS), BF),
            pltpu.VMEM((ROWS, 6 * ROWS), BF),
            pltpu.VMEM((ITERS + 1, NV, 128, E), F32),
            pltpu.VMEM((ITERS, NV, 128, E), F32),
            pltpu.VMEM((NV, 256, E), BF),
            pltpu.VMEM((NV, 384, E), F32),
            pltpu.VMEM((ROWS, COLS), F32),
            pltpu.VMEM((2 * ROWS, COLS), BF),
            pltpu.VMEM((ROWS, 4 * FS), F32),
            pltpu.VMEM((2, ROWS, IF), F32),
            pltpu.VMEM((6 * ROWS, IF), BF),
            pltpu.VMEM((2 * ROWS, IF), BF),
            pltpu.VMEM((ROWS, COLS), F32),
            pltpu.VMEM((NV, ROWS, E), F32),
            pltpu.VMEM((ITERS, 4, SEND, FS), F32),
            pltpu.VMEM((ITERS, 4, SEND, FS), F32),
            pltpu.VMEM((2, 8, 128), F32),
            pltpu.VMEM((n_span, 8, 128), F32),
            pltpu.VMEM((n_chord, 8, 128), F32),
            pltpu.SemaphoreType.DMA((ITERS, 4)),
            pltpu.SemaphoreType.DMA((ITERS, 4)),
            pltpu.SemaphoreType.DMA((n_span,)),
            pltpu.SemaphoreType.DMA((n_span,)),
            pltpu.SemaphoreType.DMA((n_chord,)),
            pltpu.SemaphoreType.DMA((n_chord,)),
        ],
        compiler_params=pltpu.CompilerParams(
            collective_id=0, has_side_effects=True, vmem_limit_bytes=48 * 1024 * 1024
        ),
    )(*args, *constants())


def solution(mesh):
    placed = (
        P(None, None, ("span", "chord")),
        P(("span", "chord")),
        P(("span", "chord")),
        P(None, None, None, ("span", "chord")),
        P(None, None, ("span", "chord")),
        P(),
        P(),
        P(("span", "chord")),
        P(None, ("span", "chord")),
        P(None, ("span", "chord")),
        P(None, ("span", "chord")),
        P(None, ("span", "chord")),
    )
    return jax.shard_map(
        functools.partial(local, mesh.shape["span"], mesh.shape["chord"]),
        mesh=mesh,
        in_specs=placed,
        out_specs=P(None, None, ("span", "chord")),
        check_vma=False,
    )
```

time: 1580 us -> 61.2 us (0.04)
  blocking collectives: 971 us -> 0 us
  local copies, waits for them, and re-layouts: 218 us -> 12.6 us
  other arithmetic: 180 us -> 0 us
  matrix products: 147 us -> 0 us
  Pallas kernels: 0 us -> 48.1 us
  starting transfers between devices: 37.7 us -> 0 us
    psum x15 -> x0, blocking collectives: 971 us -> none  [the longest x10 648 us: local(): product = lax.psum(jnp.sum(basis[position] * image), ('span', 'chord'))]
    dot_general x93 -> x0, matrix products: 147 us -> none  [the longest x12 46.7 us: volume_term(): jnp.einsum('abe,bme->ame', flux_jacobian[direction], grads[direction].res...]
    scatter-add x24 -> x0, other arithmetic: 96 us -> none  [the longest x8 42.2 us: local(): jnp.zeros_like(flat).at[:, inner_cols[0]].add(term).at[:, inner_cols[1]]]
    gather x24 -> x0, local copies, waits for them, and re-layouts: 66 us -> none  [the longest x16 40 us: local(): sides = [jnp.take(flat, side_cols[side], axis=1) for side in range(4)]]
    reshape x96 -> x0, local copies, waits for them, and re-layouts: 59.4 us -> none  [the longest x12 25.8 us: volume_term(): grads[direction].reshape(nvar, modes, count)]
    pallas_call x0 -> x1, Pallas kernels: none -> 48.1 us  [local(): pl.pallas_call(functools.partial(kernel, n_span, n_chord), out_shape=jax....]
    reduce_sum x11 -> x0, other arithmetic: 38.3 us -> none  [the longest x6 24.8 us: local(): product = lax.psum(jnp.sum(basis[position] * image), ('span', 'chord'))]
    ppermute x16 -> x0, starting transfers between devices: 37.7 us -> none  [the longest x8 21.9 us: extended(): lax.ppermute(lax.slice_in_dim(block, block.shape[dim] - width, None, axis...]
  transfers between devices with their start and end apart: 16 -> 0, of which waited for: 0 -> 0; matrix products, arithmetic and copies ran while one was open for 13% -> 0% of each run, Pallas kernels for 0% -> 0%
where the time goes in v1:
time: 61.2 us; the launch traced here: 60.7 us
  Pallas kernels  48.1 us (79%)
  local copies, waits for them, and re-layouts  12.6 us (21%)
    pallas_call x1, Pallas kernels, local(): pl.pallas_call(functools.partial(kernel, n_span, n_chord), out_shape=jax....  48.1 us
    unnamed x31, local copies, waits for them, and re-layouts  12.6 us

profile of v1, /device:TPU:1, one launch (start us, length us, event | category | flops | bytes accessed | tf_op | source)
XLA Modules:
  0.0 60.7 jit_solution(6866783183045794468)
XLA Ops:
  0.0 0.0 copy-start
  0.0 1.1 %copy-done = f32[6,125,256]{2,1,0:T(8,128)S(1)} copy-done((f32[6,125,256]{2,1,0:T(8,128)S(1)}, f32[6,125,256]{2,1,0:T(8,128)}, u32[]{:S(2)}) %copy-start) | copy-done | bytes 768024
  1.1 0.0 copy-start.1
  1.1 1.0 %copy-done.1 = bf16[544,256]{1,0:T(8,128)(2,1)S(1)} copy-done((bf16[544,256]{1,0:T(8,128)(2,1)S(1)}, bf16[544,256]{1,0:T(8,128)(2,1)}, u32[]{:S(2)}) %copy-start.1) | copy-done | bytes 278552
  2.1 0.0 copy-start.2
  2.1 0.9 %copy-done.2 = f32[3,6,6,256]{3,2,1,0:T(8,128)S(1)} copy-done((f32[3,6,6,256]{3,2,1,0:T(8,128)S(1)}, f32[3,6,6,256]{3,2,1,0:T(8,128)}, u32[]{:S(2)}) %copy-start.2) | copy-done | bytes 110616
  3.0 0.0 copy-start.3
  3.0 0.9 %copy-done.3 = bf16[128,320]{1,0:T(8,128)(2,1)S(1)} copy-done((bf16[128,320]{1,0:T(8,128)(2,1)S(1)}, bf16[128,320]{1,0:T(8,128)(2,1)}, u32[]{:S(2)}) %copy-start.3) | copy-done | bytes 81944
  3.9 0.0 copy-start.4
  3.9 0.8 %copy-done.4 = s32[128,128]{1,0:T(8,128)S(1)} copy-done((s32[128,128]{1,0:T(8,128)S(1)}, s32[128,128]{1,0:T(8,128)}, u32[]{:S(2)}) %copy-start.4) | copy-done | bytes 65560
  4.7 0.0 copy-start.5
  4.7 0.8 %copy-done.5 = f32[6,6,256]{2,1,0:T(8,128)S(1)} copy-done((f32[6,6,256]{2,1,0:T(8,128)S(1)}, f32[6,6,256]{2,1,0:T(8,128)}, u32[]{:S(2)}) %copy-start.5) | copy-done | bytes 36888
  5.5 0.0 copy-start.6
  5.5 0.7 %copy-done.6 = f32[6,6]{1,0:T(8,128)S(1)} copy-done((f32[6,6]{1,0:T(8,128)S(1)}, f32[6,6]{1,0:T(8,128)}, u32[]{:S(2)}) %copy-start.6) | copy-done | bytes 168
  6.2 0.0 copy-start.7
  6.2 0.7 %copy-done.7 = f32[6,6]{1,0:T(8,128)S(1)} copy-done((f32[6,6]{1,0:T(8,128)S(1)}, f32[6,6]{1,0:T(8,128)}, u32[]{:S(2)}) %copy-start.7) | copy-done | bytes 168
  6.9 0.0 copy-start.8
  6.9 0.7 %copy-done.8 = s32[2,512]{1,0:T(2,128)S(1)} copy-done((s32[2,512]{1,0:T(2,128)S(1)}, s32[2,512]{1,0:T(2,128)}, u32[]{:S(2)}) %copy-start.8) | copy-done | bytes 4120
  7.6 0.0 copy-start.9
  7.6 0.7 %copy-done.9 = s32[2,512]{1,0:T(2,128)S(1)} copy-done((s32[2,512]{1,0:T(2,128)S(1)}, s32[2,512]{1,0:T(2,128)}, u32[]{:S(2)}) %copy-start.9) | copy-done | bytes 4120
  8.3 0.0 copy-start.10
  8.3 0.7 %copy-done.10 = f32[512]{0:T(512)S(1)} copy-done((f32[512]{0:T(512)S(1)}, f32[512]{0:T(512)}, u32[]{:S(2)}) %copy-start.10) | copy-done | bytes 2072
  9.0 0.0 copy-start.11
  9.0 0.7 %copy-done.11 = s32[4,128]{1,0:T(4,128)S(1)} copy-done((s32[4,128]{1,0:T(4,128)S(1)}, s32[4,128]{1,0:T(4,128)}, u32[]{:S(2)}) %copy-start.11) | copy-done | bytes 2072
  9.6 0.0 copy-start.12
  9.6 0.7 %copy-done.12 = s32[4,128]{1,0:T(4,128)S(1)} copy-done((s32[4,128]{1,0:T(4,128)S(1)}, s32[4,128]{1,0:T(4,128)}, u32[]{:S(2)}) %copy-start.12) | copy-done | bytes 2072
  10.3 0.0 copy-start.13
  10.3 0.7 %copy-done.13 = s32[256]{0:T(256)S(1)} copy-done((s32[256]{0:T(256)S(1)}, s32[256]{0:T(256)}, u32[]{:S(2)}) %copy-start.13) | copy-done | bytes 1048
  11.0 0.0 copy-start.14
  11.0 0.7 %copy-done.14 = f32[256]{0:T(256)S(1)} copy-done((f32[256]{0:T(256)S(1)}, f32[256]{0:T(256)}, u32[]{:S(2)}) %copy-start.14) | copy-done | bytes 1048
  11.7 48.1 %shard_map.145 = f32[6,125,256]{2,1,0:T(8,128)S(1)} custom-call(f32[6,125,256]{2,1,0:T(8,128)S(1)} %copy-done, s32[256]{0:T(256)S(1)} %copy-done.13, f32[256]{0:T(256)S(1)} %copy-done.14, f32[3,6,6,256]{3,2,1,0:T(8,128)S(1)} %copy-done.2, f32[6,6,256]{2,1,0:T(8,128)S(1)} %copy-done.5, f32[6,6]{1,0:T(8,128)S(1)} %copy-done.6, f32[6,6]{1,0:T(8,128)S(1)} %copy-done.7, ...), custom_call_target="tpu_custom_call" | custom-call | tf_op jit(solution)/shard_map/pallas_call | solution.py:423
  59.8 0.9 %copy.17 = f32[6,125,256]{2,1,0:T(8,128)} copy(f32[6,125,256]{2,1,0:T(8,128)S(1)} %shard_map.145) | data formatting | bytes 1536000
Async XLA Ops:
  0.0 1.1 %copy-start = (f32[6,125,256]{2,1,0:T(8,128)S(1)}, f32[6,125,256]{2,1,0:T(8,128)}, u32[]{:S(2)}) copy-start(f32[6,125,256]{2,1,0:T(8,128)} %src.1) | copy-start | bytes 2304004
  1.1 1.0 %copy-start.1 = (bf16[544,256]{1,0:T(8,128)(2,1)S(1)}, bf16[544,256]{1,0:T(8,128)(2,1)}, u32[]{:S(2)}) copy-start(bf16[544,256]{1,0:T(8,128)(2,1)} %constant.6.clone.mode_mat) | copy-start | bytes 835588
  2.1 0.9 %copy-start.2 = (f32[3,6,6,256]{3,2,1,0:T(8,128)S(1)}, f32[3,6,6,256]{3,2,1,0:T(8,128)}, u32[]{:S(2)}) copy-start(f32[3,6,6,256]{3,2,1,0:T(8,128)} %jac.1) | copy-start | bytes 331780
  3.0 0.9 %copy-start.3 = (bf16[128,320]{1,0:T(8,128)(2,1)S(1)}, bf16[128,320]{1,0:T(8,128)(2,1)}, u32[]{:S(2)}) copy-start(bf16[128,320]{1,0:T(8,128)(2,1)} %constant.7.clone.lift_mat) | copy-start | bytes 245764
  3.9 0.8 %copy-start.4 = (s32[128,128]{1,0:T(8,128)S(1)}, s32[128,128]{1,0:T(8,128)}, u32[]{:S(2)}) copy-start(s32[128,128]{1,0:T(8,128)} %constant.8.clone.highest) | copy-start | bytes 196612
  4.7 0.8 %copy-start.5 = (f32[6,6,256]{2,1,0:T(8,128)S(1)}, f32[6,6,256]{2,1,0:T(8,128)}, u32[]{:S(2)}) copy-start(f32[6,6,256]{2,1,0:T(8,128)} %binv.1) | copy-start | bytes 110596
  5.5 0.7 %copy-start.6 = (f32[6,6]{1,0:T(8,128)S(1)}, f32[6,6]{1,0:T(8,128)}, u32[]{:S(2)}) copy-start(f32[6,6]{1,0:T(8,128)} %diss.1) | copy-start | bytes 436
  6.2 0.7 %copy-start.7 = (f32[6,6]{1,0:T(8,128)S(1)}, f32[6,6]{1,0:T(8,128)}, u32[]{:S(2)}) copy-start(f32[6,6]{1,0:T(8,128)} %conv.1) | copy-start | bytes 436
  6.9 0.7 %copy-start.8 = (s32[2,512]{1,0:T(2,128)S(1)}, s32[2,512]{1,0:T(2,128)}, u32[]{:S(2)}) copy-start(s32[2,512]{1,0:T(2,128)} %face_el.1) | copy-start | bytes 12292
  7.6 0.7 %copy-start.9 = (s32[2,512]{1,0:T(2,128)S(1)}, s32[2,512]{1,0:T(2,128)}, u32[]{:S(2)}) copy-start(s32[2,512]{1,0:T(2,128)} %face_no.1) | copy-start | bytes 12292
  8.3 0.7 %copy-start.10 = (f32[512]{0:T(512)S(1)}, f32[512]{0:T(512)}, u32[]{:S(2)}) copy-start(f32[512]{0:T(512)} %weight.1) | copy-start | bytes 6148
  9.0 0.7 %copy-start.11 = (s32[4,128]{1,0:T(4,128)S(1)}, s32[4,128]{1,0:T(4,128)}, u32[]{:S(2)}) copy-start(s32[4,128]{1,0:T(4,128)} %side_el.1) | copy-start | bytes 6148
  9.6 0.7 %copy-start.12 = (s32[4,128]{1,0:T(4,128)S(1)}, s32[4,128]{1,0:T(4,128)}, u32[]{:S(2)}) copy-start(s32[4,128]{1,0:T(4,128)} %side_no.1) | copy-start | bytes 6148
  10.3 0.7 %copy-start.13 = (s32[256]{0:T(256)S(1)}, s32[256]{0:T(256)}, u32[]{:S(2)}) copy-start(s32[256]{0:T(256)} %degrees.1) | copy-start | bytes 3076
  11.0 0.7 %copy-start.14 = (f32[256]{0:T(256)S(1)}, f32[256]{0:T(256)}, u32[]{:S(2)}) copy-start(f32[256]{0:T(256)} %time_shift.1) | copy-start | bytes 3076

commit v2 on v1

--- a/solution.py
+++ b/solution.py
@@ -19,6 +19,7 @@
 COLS = NF * E
 SLOTS = 2 * IF + 4 * FS
 SHIFT = 1.5
+LOAD_ORDER = (8, 9, 10, 11, 0, 1, 4, 12, 3, 5, 6, 7, 2, 13)
 MESH = pl.DeviceIdType.MESH
 BF = jnp.bfloat16
 F32 = jnp.float32
@@ -49,13 +50,9 @@
                         if (idx[d] - low) % 2 == 1:
                             out = m - step[d] * (idx[d] - low)
                             mode_mat[ROWS + 128 * d + out, m] = 2 * low + 1
-    highest = np.full((128, 128), 99, np.int32)
-    for m in range(125):
-        highest[m] = max(m // 25, m // 5 % 5, m % 5)
     return (
-        jnp.asarray(np.concatenate([mode_mat, mode_mat], axis=1), BF),
-        jnp.asarray(np.concatenate([lift, lift], axis=1), BF),
-        jnp.asarray(highest),
+        jnp.asarray(mode_mat),
+        jnp.asarray(np.concatenate([lift, lift], axis=1)),
     )
 
 
@@ -75,50 +72,65 @@
 def kernel(
     n_span,
     n_chord,
-    src,
-    degrees,
-    time_shift,
-    jac,
-    binv,
-    diss,
-    conv,
-    weight,
-    face_el,
-    face_no,
-    side_el,
-    side_no,
-    mode_mat,
-    lift_mat,
-    highest,
-    out,
-    active,
-    jac2,
-    select,
-    mix,
-    us,
-    zs,
-    modes,
-    grads,
-    flat,
-    flat_b,
-    own,
-    interior,
-    uv_b,
-    term_b,
-    gathered,
-    faces,
-    sends,
-    recvs,
-    gram,
-    red1,
-    red2,
-    send_sem,
-    recv_sem,
-    r1_send,
-    r1_recv,
-    r2_send,
-    r2_recv,
+    *refs,
 ):
+    operands, (out,), refs = refs[:14], refs[14:15], refs[15:]
+    held, load_sem, refs = refs[:14], refs[14], refs[15:]
+    (
+        src,
+        degrees,
+        time_shift,
+        jac,
+        binv,
+        diss,
+        conv,
+        weight,
+        face_el,
+        face_no,
+        side_el,
+        side_no,
+        mode_in,
+        lift_in,
+    ) = held
+    (
+        mode_mat,
+        lift_mat,
+        active,
+        jac2,
+        select,
+        mix,
+        us,
+        zs,
+        modes,
+        grads,
+        flat,
+        flat_b,
+        own,
+        interior,
+        uv_b,
+        term_b,
+        gathered,
+        faces,
+        sends,
+        recvs,
+        gram,
+        red1,
+        red2,
+        send_sem,
+        recv_sem,
+        r1_send,
+        r1_recv,
+        r2_send,
+        r2_recv,
+    ) = refs
+    loads = [pltpu.make_async_copy(a, b, load_sem.at[k]) for k, (a, b) in enumerate(zip(operands, held))]
+    for k in LOAD_ORDER:
+        loads[k].start()
+
+    def arrived(*which):
+        for k in which:
+            loads[k].wait()
+
     span = lax.axis_index("span")
     chord = lax.axis_index("chord")
 
@@ -135,13 +147,7 @@
     has = (span > 0, span < n_span - 1, chord > 0, chord < n_chord - 1)
     targets = ((span - 1, chord), (span + 1, chord), (span, chord - 1), (span, chord + 1))
 
-    act = (highest[:, 0:1] <= degrees[...].reshape(1, E)).astype(F32)
-    active[...] = act
-    for b in range(NV):
-        us[0, b, 125:128, :] = jnp.zeros((3, E), F32)
-        us[0, b, 0:125, :] = src[b] * act[0:125]
-    jac2[...] = jac[...] * 0.2
-
+    arrived(8, 9, 10, 11)
     cols_in = face_no[...] * E + face_el[...]
     cols_sd = side_no[...] * E + side_el[...]
     left = cols_in[0:1, :]
@@ -160,7 +166,27 @@
             select[pl.ds(base, 16), 2 * IF + q * FS : 2 * IF + (q + 1) * FS] = s.astype(BF)
         return carry
 
-    lax.fori_loop(0, COLS // 16, build, 0)
+    lax.fori_loop(0, COLS // 16, build, 0, unroll=4)
+
+    arrived(0, 1, 3, 5, 6)
+    mode = lax.broadcasted_iota(jnp.int32, (128, 128), 0)
+
+    def digit(x, unit):
+        return sum((x >= unit * k).astype(jnp.int32) for k in range(1, 5))
+
+    first = digit(mode, 25)
+    second = digit(mode - 25 * first, 5)
+    third = mode - 25 * first - 5 * second
+    highest = jnp.maximum(jnp.maximum(first, second), third)
+    highest = jnp.where(mode < 125, highest, 99)
+    for lt in range(2):
+        lanes = slice(lt * 128, (lt + 1) * 128)
+        act = (highest <= degrees[...].reshape(1, E)[:, lanes]).astype(F32)
+        active[:, lanes] = act
+        for b in range(NV):
+            us[0, b, 125:128, lanes] = jnp.zeros((3, 128), F32)
+            us[0, b, 0:125, lanes] = src[b, :, lanes] * act[0:125]
+    jac2[...] = jac[...] * 0.2
 
     r24 = lax.broadcasted_iota(jnp.int32, (24, ROWS), 0)
     c24 = lax.broadcasted_iota(jnp.int32, (24, ROWS), 1)
@@ -195,6 +221,10 @@
             for k in range(ITERS):
                 recvs[k, s] = jnp.zeros((SEND, FS), F32)
 
+    arrived(2, 4, 7, 12, 13)
+    mode_mat[:, 0:128] = mode_in[...].astype(BF)
+    mode_mat[:, 128:256] = mode_in[...].astype(BF)
+    lift_mat[...] = lift_in[...].astype(BF)
     pl.semaphore_wait(barrier, n_span + n_chord - 2)
 
     def side_copy(step, s):
@@ -416,16 +446,18 @@
 
 
 def local(n_span, n_chord, *args):
-    vmem = pl.BlockSpec(memory_space=pltpu.VMEM)
-    smem = pl.BlockSpec(memory_space=pltpu.SMEM)
-    specs = [vmem] * 15
-    specs[5] = specs[6] = smem
+    args = args + constants()
+    held = [(pltpu.SMEM if k in (5, 6) else pltpu.VMEM)(a.shape, a.dtype) for k, a in enumerate(args)]
     return pl.pallas_call(
         functools.partial(kernel, n_span, n_chord),
         out_shape=jax.ShapeDtypeStruct((NV, 125, E), F32),
-        in_specs=specs,
-        out_specs=vmem,
-        scratch_shapes=[
+        in_specs=[pl.BlockSpec(memory_space=pltpu.HBM)] * len(args),
+        out_specs=pl.BlockSpec(memory_space=pltpu.VMEM),
+        scratch_shapes=held
+        + [
+            pltpu.SemaphoreType.DMA((len(args),)),
+            pltpu.VMEM((ROWS + 384, 256), BF),
+            pltpu.VMEM((128, 2 * ROWS), BF),
             pltpu.VMEM((128, E), F32),
             pltpu.VMEM((3, NV, NV, E), F32),
             pltpu.VMEM((COLS, SLOTS), BF),
@@ -455,9 +487,9 @@
             pltpu.SemaphoreType.DMA((n_chord,)),
         ],
         compiler_params=pltpu.CompilerParams(
-            collective_id=0, has_side_effects=True, vmem_limit_bytes=48 * 1024 * 1024
+            collective_id=0, has_side_effects=True, vmem_limit_bytes=60 * 1024 * 1024
         ),
-    )(*args, *constants())
+    )(*args)
 
 
 def solution(mesh):

time: 61.2 us -> 50.6 us (0.83)
  local copies, waits for them, and re-layouts: 12.6 us -> 2.1 us
    unnamed x31 -> x1, local copies, waits for them, and re-layouts: 12.6 us -> 2.1 us
where the time goes in v2:
time: 50.6 us; the launch traced here: 50.4 us
  Pallas kernels  48.3 us (95%)
  local copies, waits for them, and re-layouts  2.1 us (4%)
    pallas_call x1, Pallas kernels, local(): pl.pallas_call(functools.partial(kernel, n_span, n_chord), out_shape=jax....  48.3 us
    unnamed x1, local copies, waits for them, and re-layouts  2.1 us

profile of v2, /device:TPU:1, one launch (start us, length us, event | category | flops | bytes accessed | tf_op | source)
XLA Modules:
  0.0 50.4 jit_solution(6163643482440441447)
XLA Ops:
  0.0 48.3 %shard_map.136 = f32[6,125,256]{2,1,0:T(8,128)} custom-call(f32[6,125,256]{2,1,0:T(8,128)} %refs_0_.1, s32[256]{0:T(256)} %refs_1_.1, f32[256]{0:T(256)} %refs_2_.1, f32[3,6,6,256]{3,2,1,0:T(8,128)} %refs_3_.1, f32[6,6,256]{2,1,0:T(8,128)} %refs_4_.1, f32[6,6]{1,0:T(8,128)} %refs_5_.1, f32[6,6]{1,0:T(8,128)} %refs_6_.1, f32[512]{0:T(512)} %refs_7_.1, ...), custom_call_target="tpu_custom_call" | custom-call | tf_op jit(solution)/shard_map/pallas_call | solution.py:451
  48.3 2.1 %copy.16 = f32[6,125,256]{2,1,0:T(8,128)} copy(f32[6,125,256]{2,1,0:T(8,128)} %shard_map.136) | data formatting | bytes 1536000

commit v3 on v2

--- a/solution.py
+++ b/solution.py
@@ -19,7 +19,9 @@
 COLS = NF * E
 SLOTS = 2 * IF + 4 * FS
 SHIFT = 1.5
+FULL_STEPS = 2
 LOAD_ORDER = (8, 9, 10, 11, 0, 1, 4, 12, 3, 5, 6, 7, 2, 13)
+STAGES = (("span", 1, 8), ("chord", 1, 16))
 MESH = pl.DeviceIdType.MESH
 BF = jnp.bfloat16
 F32 = jnp.float32
@@ -74,7 +76,7 @@
     n_chord,
     *refs,
 ):
-    operands, (out,), refs = refs[:14], refs[14:15], refs[15:]
+    operands, out, refs = refs[:14], refs[14], refs[15:]
     held, load_sem, refs = refs[:14], refs[14], refs[15:]
     (
         src,
@@ -106,7 +108,6 @@
         flat,
         flat_b,
         own,
-        interior,
         uv_b,
         term_b,
         gathered,
@@ -114,14 +115,11 @@
         sends,
         recvs,
         gram,
-        red1,
-        red2,
+        sums_in,
         send_sem,
         recv_sem,
-        r1_send,
-        r1_recv,
-        r2_send,
-        r2_recv,
+        sum_send,
+        sum_recv,
     ) = refs
     loads = [pltpu.make_async_copy(a, b, load_sem.at[k]) for k, (a, b) in enumerate(zip(operands, held))]
     for k in LOAD_ORDER:
@@ -135,17 +133,25 @@
     chord = lax.axis_index("chord")
 
     barrier = pltpu.get_barrier_semaphore()
-    for i in range(1, n_span):
-        pl.semaphore_signal(
-            barrier, inc=1, device_id=(lax.rem(span + i, n_span), chord), device_id_type=MESH
-        )
-    for i in range(1, n_chord):
-        pl.semaphore_signal(
-            barrier, inc=1, device_id=(span, lax.rem(chord + i, n_chord)), device_id_type=MESH
-        )
+    def partner(stage, i):
+        axis, stride, size = STAGES[stage]
+        index = span if axis == "span" else chord
+        digit = lax.rem(index // stride, size)
+        index = index + (lax.rem(digit + i, size) - digit) * stride
+        return (index, chord) if axis == "span" else (span, index)
+
+    partners = [(k, i) for k, stage in enumerate(STAGES) for i in range(1, stage[2])]
+    for k, i in partners:
+        pl.semaphore_signal(barrier, inc=1, device_id=partner(k, i), device_id_type=MESH)
 
     has = (span > 0, span < n_span - 1, chord > 0, chord < n_chord - 1)
-    targets = ((span - 1, chord), (span + 1, chord), (span, chord - 1), (span, chord + 1))
+    has = [h.astype(F32) for h in has]
+    targets = (
+        (lax.rem(span + n_span - 1, n_span), chord),
+        (lax.rem(span + 1, n_span), chord),
+        (span, lax.rem(chord + n_chord - 1, n_chord)),
+        (span, lax.rem(chord + 1, n_chord)),
+    )
 
     arrived(8, 9, 10, 11)
     cols_in = face_no[...] * E + face_el[...]
@@ -161,8 +167,8 @@
             l = (rows == left[:, q * FS : (q + 1) * FS]).astype(F32)
             r = (rows == right[:, q * FS : (q + 1) * FS]).astype(F32)
             s = (rows == cols_sd[q : q + 1, :]).astype(F32)
-            select[pl.ds(base, 16), q * FS : (q + 1) * FS] = (l - r).astype(BF)
-            select[pl.ds(base, 16), IF + q * FS : IF + (q + 1) * FS] = (l + r).astype(BF)
+            select[pl.ds(base, 16), IF + q * FS : IF + (q + 1) * FS] = (l - r).astype(BF)
+            select[pl.ds(base, 16), q * FS : (q + 1) * FS] = (l + r).astype(BF)
             select[pl.ds(base, 16), 2 * IF + q * FS : 2 * IF + (q + 1) * FS] = s.astype(BF)
         return carry
 
@@ -214,18 +220,11 @@
 
     flat[...] = jnp.zeros_like(flat)
     faces[...] = jnp.zeros_like(faces)
-    for s in range(4):
-
-        @pl.when(jnp.logical_not(has[s]))
-        def _(s=s):
-            for k in range(ITERS):
-                recvs[k, s] = jnp.zeros((SEND, FS), F32)
-
     arrived(2, 4, 7, 12, 13)
     mode_mat[:, 0:128] = mode_in[...].astype(BF)
     mode_mat[:, 128:256] = mode_in[...].astype(BF)
     lift_mat[...] = lift_in[...].astype(BF)
-    pl.semaphore_wait(barrier, n_span + n_chord - 2)
+    pl.semaphore_wait(barrier, len(partners))
 
     def side_copy(step, s):
         return pltpu.make_async_remote_copy(
@@ -237,18 +236,30 @@
             device_id_type=MESH,
         )
 
-    def mix_terms(difference, total):
+    def mix_terms(difference, total, full):
+        n = difference.shape[1]
         d_hi, d_lo = split(difference)
         t_hi, t_lo = split(total)
-        n = difference.shape[1]
-        for k, part in enumerate((d_hi, t_hi, d_lo, t_lo, d_hi, t_hi)):
+        parts = (d_hi, t_hi, d_lo, t_lo, d_hi, t_hi) if full else (d_hi, t_hi)
+        for k, part in enumerate(parts):
             uv_b[k * ROWS : (k + 1) * ROWS, 0:n] = part
-        return dot(mix[...], uv_b[:, 0:n])
-
-    def one_step(step, carry):
-        for lt in range(2):
-            lanes = slice(lt * 128, (lt + 1) * 128)
-            for a0 in range(0, NV, 2):
+        return dot(mix[:, 0 : len(parts) * ROWS], uv_b[0 : len(parts) * ROWS, 0:n])
+
+    def store_parts(ref, x, row, cols, full):
+        hi, lo = split(x)
+        n = x.shape[0]
+        ref[row : row + n, cols] = hi
+        if full:
+            ref[ROWS + row : ROWS + row + n, cols] = lo
+
+    def both(t, full):
+        return t[0:ROWS] + t[ROWS:] if full else t
+
+    def one_step(full, step, carry):
+        used = 2 * ROWS if full else ROWS
+        for a0 in range(0, NV, 2):
+            for lt in range(2):
+                lanes = slice(lt * 128, (lt + 1) * 128)
                 acc = [None, None]
                 for b in range(NV):
                     u = us[step, b, :, lanes]
@@ -260,83 +271,89 @@
                     hi, lo = split(acc[p])
                     modes[a0 + p, 0:128, lanes] = hi
                     modes[a0 + p, 128:256, lanes] = lo
-        for b in range(NV):
-            t = dot(mode_mat[0:ROWS, :], modes[b])
-            for f in range(NF):
-                flat[b * 24 : (b + 1) * 24, f * E : (f + 1) * E] = t[f * 24 : (f + 1) * 24]
-                flat[144 + b : 145 + b, f * E : (f + 1) * E] = t[144 + f : 145 + f]
-        for f in range(NF):
-            hi, lo = split(flat[:, f * E : (f + 1) * E])
-            flat_b[0:ROWS, f * E : (f + 1) * E] = hi
-            flat_b[ROWS : 2 * ROWS, f * E : (f + 1) * E] = lo
-        t = dot(flat_b[...], select[:, 2 * IF :])
-        own[...] = t[0:ROWS] + t[ROWS:]
-        for s in range(4):
-            sends[step, s] = own[0:SEND, s * FS : (s + 1) * FS]
-
-            @pl.when(has[s])
-            def _(s=s):
+            for b in (a0, a0 + 1):
+                t = dot(mode_mat[0:ROWS, :], modes[b])
+                for f in range(NF):
+                    cols = slice(f * E, (f + 1) * E)
+                    flat[b * 24 : (b + 1) * 24, cols] = t[f * 24 : (f + 1) * 24]
+                    flat[144 + b : 145 + b, cols] = t[144 + f : 145 + f]
+            store_parts(flat_b, flat[a0 * 24 : (a0 + 2) * 24, :], a0 * 24, slice(0, COLS), full)
+        store_parts(flat_b, flat[144:ROWS, :], 144, slice(0, COLS), full)
+        for pair in (1, 0):
+            cols = slice(2 * IF + pair * 2 * FS, 2 * IF + (pair + 1) * 2 * FS)
+            t = both(dot(flat_b[0:used], select[:, cols]), full)
+            own[:, pair * 2 * FS : (pair + 1) * 2 * FS] = t
+            for s in (2 * pair, 2 * pair + 1):
+                sends[step, s] = t[0:SEND, (s % 2) * FS : (s % 2 + 1) * FS]
                 side_copy(step, s).start()
 
         for b in range(NV):
             grads[b] = dot(mode_mat[ROWS:, :], modes[b])
-        for q in range(2):
-            t = dot(flat_b[...], select[:, q * IF : (q + 1) * IF])
-            interior[q] = t[0:ROWS] + t[ROWS:]
-        term = mix_terms(interior[0], interior[1]) * weight[...].reshape(1, IF)
-        hi, lo = split(term)
-        term_b[0:ROWS] = hi
-        term_b[ROWS:] = lo
-        for f in range(NF):
-            t = dot_t(term_b[...], select[f * E : (f + 1) * E, 0:IF])
-            gathered[:, f * E : (f + 1) * E] = t[0:ROWS] + t[ROWS:]
-        for lt in range(2):
+        def volume(a0, lt):
             lanes = slice(lt * 128, (lt + 1) * 128)
             shift = time_shift[...].reshape(1, E)[:, lanes]
-            for a0 in range(0, NV, 2):
-                acc = [shift * zs[step, a0 + p, :, lanes] for p in range(2)]
-                for d in range(3):
-                    for b in range(NV):
-                        g = grads[b, d * 128 : (d + 1) * 128, lanes]
-                        for p in range(2):
-                            acc[p] = acc[p] + jac2[d, a0 + p, b : b + 1, lanes] * g
-                for p in range(2):
-                    us[step + 1, a0 + p, :, lanes] = acc[p]
-        for s in range(4):
-
-            @pl.when(has[s])
-            def _(s=s):
+            acc = [shift * zs[step, a0 + p, :, lanes] for p in range(2)]
+            for d in range(3):
+                for b in range(NV):
+                    g = grads[b, d * 128 : (d + 1) * 128, lanes]
+                    for p in range(2):
+                        acc[p] = acc[p] + jac2[d, a0 + p, b : b + 1, lanes] * g
+            for p in range(2):
+                us[step + 1, a0 + p, :, lanes] = acc[p]
+
+        volumes = [functools.partial(volume, a0, lt) for lt in range(2) for a0 in range(0, NV, 2)]
+
+        for q in range(2):
+            cols = slice(q * E, (q + 1) * E)
+            total = both(dot(flat_b[0:used], select[:, cols]), full)
+            volumes.pop()()
+            difference = both(dot(flat_b[0:used], select[:, IF + q * E : IF + (q + 1) * E]), full)
+            volumes.pop()()
+            term = mix_terms(difference, total, full) * weight[...].reshape(1, IF)[:, cols]
+            store_parts(term_b, term, 0, cols, full)
+            volumes.pop()()
+
+        def side_terms(pair):
+            diffs, totals = [], []
+            for s in (2 * pair, 2 * pair + 1):
                 side_copy(step, s ^ 1).wait_recv()
-
-        diffs, sums = [], []
-        for s in range(4):
-            mine = own[:, s * FS : (s + 1) * FS]
-            other = jnp.concatenate([recvs[step, s], jnp.zeros((ROWS - SEND, FS), F32)], axis=0)
-            diffs.append(mine - other)
-            sums.append(mine + other if s % 2 == 1 else -(mine + other))
-        term = mix_terms(jnp.concatenate(diffs, axis=1), jnp.concatenate(sums, axis=1))
-        hi, lo = split(term)
-        term_b[0:ROWS] = hi
-        term_b[ROWS:] = lo
+                mine = own[:, s * FS : (s + 1) * FS]
+                other = recvs[step, s] * has[s]
+                other = jnp.concatenate([other, jnp.zeros((ROWS - SEND, FS), F32)], axis=0)
+                diffs.append(mine - other)
+                totals.append(mine + other if s % 2 == 1 else -(mine + other))
+            term = mix_terms(jnp.concatenate(diffs, axis=1), jnp.concatenate(totals, axis=1), full)
+            start = IF + pair * 2 * FS
+            store_parts(term_b, term, 0, slice(start, start + 2 * FS), full)
+
+        def scattered(f, start, stop):
+            return both(
+                dot_t(term_b[0:used, start:stop], select[f * E : (f + 1) * E, IF + start : IF + stop]),
+                full,
+            )
+
+        side_terms(0)
         for f in range(NF):
-            t = dot_t(term_b[...], select[f * E : (f + 1) * E, 2 * IF :])
-            t = gathered[:, f * E : (f + 1) * E] + (t[0:ROWS] + t[ROWS:])
+            gathered[:, f * E : (f + 1) * E] = scattered(f, 0, IF + 2 * FS)
+        side_terms(1)
+        for f in range(NF):
+            t = gathered[:, f * E : (f + 1) * E] + scattered(f, IF + 2 * FS, IF + 4 * FS)
             for b in range(NV):
                 faces[b, f * 24 : (f + 1) * 24, :] = t[b * 24 : (b + 1) * 24]
                 faces[b, 144 + f : 145 + f, :] = t[144 + b : 145 + b]
         for b in range(NV):
             hi, lo = split(faces[b])
-            t = dot(lift_mat[...], jnp.concatenate([hi, lo], axis=0))
+            if full:
+                t = dot(lift_mat[...], jnp.concatenate([hi, lo], axis=0))
+            else:
+                t = dot(lift_mat[:, 0:ROWS], hi)
             us[step + 1, b] = (us[step + 1, b] + t) * active[...] - SHIFT * us[step, b]
         for s in range(4):
-
-            @pl.when(has[s])
-            def _(s=s):
-                side_copy(step, s).wait_send()
-
+            side_copy(step, s).wait_send()
         return carry
 
-    lax.fori_loop(0, ITERS, one_step, 0)
+    lax.fori_loop(0, FULL_STEPS, functools.partial(one_step, True), 0)
+    lax.fori_loop(FULL_STEPS, ITERS, functools.partial(one_step, False), 0)
 
     pairs = [(i, j) for i in range(ITERS + 1) for j in range(i, ITERS + 1)]
 
@@ -362,39 +379,25 @@
     x = jnp.sum(jnp.where((lane >= row * 8) & (lane < row * 8 + 8), x, 0.0), axis=0, keepdims=True)
     gram[0] = jnp.broadcast_to(x, (8, 128))
 
-    def r1_copy(i):
+    def sum_copy(k, i):
         return pltpu.make_async_remote_copy(
-            src_ref=gram.at[0],
-            dst_ref=red1.at[i],
-            send_sem=r1_send.at[i],
-            recv_sem=r1_recv.at[i],
-            device_id=(lax.rem(span + i, n_span), chord),
+            src_ref=gram.at[k],
+            dst_ref=sums_in.at[k, i],
+            send_sem=sum_send.at[k, i],
+            recv_sem=sum_recv.at[k, i],
+            device_id=partner(k, i),
             device_id_type=MESH,
         )
 
-    def r2_copy(i):
-        return pltpu.make_async_remote_copy(
-            src_ref=gram.at[1],
-            dst_ref=red2.at[i],
-            send_sem=r2_send.at[i],
-            recv_sem=r2_recv.at[i],
-            device_id=(span, lax.rem(chord + i, n_chord)),
-            device_id_type=MESH,
-        )
-
-    for i in range(1, n_span):
-        r1_copy(i).start()
     total = gram[0]
-    for i in range(1, n_span):
-        r1_copy(i).wait_recv()
-        total = total + red1[i]
-    gram[1] = total
-    for i in range(1, n_chord):
-        r2_copy(i).start()
-    total = gram[1]
-    for i in range(1, n_chord):
-        r2_copy(i).wait_recv()
-        total = total + red2[i]
+    for k, (_, _, size) in enumerate(STAGES):
+        if k > 0:
+            gram[k] = total
+        for i in range(1, size):
+            sum_copy(k, i).start()
+        for i in range(1, size):
+            sum_copy(k, i).wait_recv()
+            total = total + sums_in[k, i]
     for amount in (4, 2, 1):
         total = total + pltpu.roll(total, 128 - amount, 1)
 
@@ -430,23 +433,19 @@
     for i in reversed(range(ITERS)):
         for k in range(i + 1, ITERS):
             coeffs[i] = coeffs[i] - low[k][i] * coeffs[k]
-    coeffs = [c[0:1, :] for c in coeffs]
     for b in range(NV):
         for lt in range(2):
             lanes = slice(lt * 128, (lt + 1) * 128)
-            x = coeffs[0] * zs[0, b, 0:125, lanes]
+            x = coeffs[0][0:1] * zs[0, b, 0:125, lanes]
             for k in range(1, ITERS):
-                x = x + coeffs[k] * zs[k, b, 0:125, lanes]
+                x = x + coeffs[k][0:1] * zs[k, b, 0:125, lanes]
             out[b, :, lanes] = x
-
-    for i in range(1, n_span):
-        r1_copy(i).wait_send()
-    for i in range(1, n_chord):
-        r2_copy(i).wait_send()
+    for k, i in partners:
+        sum_copy(k, i).wait_send()
 
 
 def local(n_span, n_chord, *args):
-    args = args + constants()
+    args = tuple(pltpu.with_memory_space_constraint(a, pltpu.HBM) for a in args + constants())
     held = [(pltpu.SMEM if k in (5, 6) else pltpu.VMEM)(a.shape, a.dtype) for k, a in enumerate(args)]
     return pl.pallas_call(
         functools.partial(kernel, n_span, n_chord),
@@ -469,25 +468,21 @@
             pltpu.VMEM((ROWS, COLS), F32),
             pltpu.VMEM((2 * ROWS, COLS), BF),
             pltpu.VMEM((ROWS, 4 * FS), F32),
-            pltpu.VMEM((2, ROWS, IF), F32),
             pltpu.VMEM((6 * ROWS, IF), BF),
-            pltpu.VMEM((2 * ROWS, IF), BF),
+            pltpu.VMEM((2 * ROWS, IF + 4 * FS), BF),
             pltpu.VMEM((ROWS, COLS), F32),
             pltpu.VMEM((NV, ROWS, E), F32),
             pltpu.VMEM((ITERS, 4, SEND, FS), F32),
             pltpu.VMEM((ITERS, 4, SEND, FS), F32),
-            pltpu.VMEM((2, 8, 128), F32),
-            pltpu.VMEM((n_span, 8, 128), F32),
-            pltpu.VMEM((n_chord, 8, 128), F32),
+            pltpu.VMEM((len(STAGES), 8, 128), F32),
+            pltpu.VMEM((len(STAGES), 16, 8, 128), F32),
             pltpu.SemaphoreType.DMA((ITERS, 4)),
             pltpu.SemaphoreType.DMA((ITERS, 4)),
-            pltpu.SemaphoreType.DMA((n_span,)),
-            pltpu.SemaphoreType.DMA((n_span,)),
-            pltpu.SemaphoreType.DMA((n_chord,)),
-            pltpu.SemaphoreType.DMA((n_chord,)),
+            pltpu.SemaphoreType.DMA((len(STAGES), 16)),
+            pltpu.SemaphoreType.DMA((len(STAGES), 16)),
         ],
         compiler_params=pltpu.CompilerParams(
-            collective_id=0, has_side_effects=True, vmem_limit_bytes=60 * 1024 * 1024
+            collective_id=0, has_side_effects=True, vmem_limit_bytes=44 * 1024 * 1024
         ),
     )(*args)
 

time: 50.6 us -> 49.4 us (0.976)
  local copies, waits for them, and re-layouts: 2.1 us -> 0.88 us
    unnamed x1, local copies, waits for them, and re-layouts: 2.1 us -> 0.88 us
where the time goes in v3:
time: 49.4 us; the launch traced here: 49.2 us
  Pallas kernels  48.4 us (98%)
  local copies, waits for them, and re-layouts  0.88 us (2%)
    pallas_call x1, Pallas kernels, local(): pl.pallas_call(functools.partial(kernel, n_span, n_chord), out_shape=jax....  48.4 us

profile of v3, /device:TPU:1, one launch (start us, length us, event | category | flops | bytes accessed | tf_op | source)
XLA Modules:
  0.0 49.2 jit_solution(7839681600774709920)
XLA Ops:
  0.0 48.4 %shard_map.136 = f32[6,125,256]{2,1,0:T(8,128)S(1)} custom-call(f32[6,125,256]{2,1,0:T(8,128)} %refs_0_.1, s32[256]{0:T(256)} %refs_1_.1, f32[256]{0:T(256)} %refs_2_.1, f32[3,6,6,256]{3,2,1,0:T(8,128)} %refs_3_.1, f32[6,6,256]{2,1,0:T(8,128)} %refs_4_.1, f32[6,6]{1,0:T(8,128)} %refs_5_.1, f32[6,6]{1,0:T(8,128)} %refs_6_.1, f32[512]{0:T(512)} %refs_7_.1, ...), custom_call_target="tpu_custom_call" | custom-call | tf_op jit(solution)/shard_map/pallas_call | solution.py:450
  48.4 0.9 %copy.16 = f32[6,125,256]{2,1,0:T(8,128)} copy(f32[6,125,256]{2,1,0:T(8,128)S(1)} %shard_map.136) | data formatting | bytes 1536000

commit v4 on v3

--- a/solution.py
+++ b/solution.py
@@ -107,7 +107,6 @@
         grads,
         flat,
         flat_b,
-        own,
         uv_b,
         term_b,
         gathered,
@@ -120,6 +119,7 @@
         recv_sem,
         sum_send,
         sum_recv,
+        prods,
     ) = refs
     loads = [pltpu.make_async_copy(a, b, load_sem.at[k]) for k, (a, b) in enumerate(zip(operands, held))]
     for k in LOAD_ORDER:
@@ -237,13 +237,12 @@
         )
 
     def mix_terms(difference, total, full):
-        n = difference.shape[1]
         d_hi, d_lo = split(difference)
         t_hi, t_lo = split(total)
         parts = (d_hi, t_hi, d_lo, t_lo, d_hi, t_hi) if full else (d_hi, t_hi)
         for k, part in enumerate(parts):
-            uv_b[k * ROWS : (k + 1) * ROWS, 0:n] = part
-        return dot(mix[:, 0 : len(parts) * ROWS], uv_b[0 : len(parts) * ROWS, 0:n])
+            uv_b[k * ROWS : (k + 1) * ROWS, :] = part
+        return dot(mix[:, 0 : len(parts) * ROWS], uv_b[0 : len(parts) * ROWS, :])
 
     def store_parts(ref, x, row, cols, full):
         hi, lo = split(x)
@@ -254,6 +253,24 @@
 
     def both(t, full):
         return t[0:ROWS] + t[ROWS:] if full else t
+
+    early = [(i, j) for i in range(ITERS) for j in range(i, ITERS)]
+
+    def early_products():
+        def products(c, accs):
+            accs = list(accs)
+            base = pl.multiple_of(c * 8, 8)
+            for b in range(NV):
+                for lt in range(2):
+                    lanes = slice(lt * 128, (lt + 1) * 128)
+                    v = [us[k, b, pl.ds(base, 8), lanes] for k in range(ITERS)]
+                    for n, (i, j) in enumerate(early):
+                        accs[n] = accs[n] + v[i] * v[j]
+            return tuple(accs)
+
+        accs = lax.fori_loop(0, 16, products, (jnp.zeros((8, 128), F32),) * len(early))
+        for n, acc in enumerate(accs):
+            prods[n] = acc
 
     def one_step(full, step, carry):
         used = 2 * ROWS if full else ROWS
@@ -282,7 +299,6 @@
         for pair in (1, 0):
             cols = slice(2 * IF + pair * 2 * FS, 2 * IF + (pair + 1) * 2 * FS)
             t = both(dot(flat_b[0:used], select[:, cols]), full)
-            own[:, pair * 2 * FS : (pair + 1) * 2 * FS] = t
             for s in (2 * pair, 2 * pair + 1):
                 sends[step, s] = t[0:SEND, (s % 2) * FS : (s % 2 + 1) * FS]
                 side_copy(step, s).start()
@@ -313,16 +329,20 @@
             store_parts(term_b, term, 0, cols, full)
             volumes.pop()()
 
+        if not full:
+            pl.when(step == ITERS - 1)(early_products)
         def side_terms(pair):
             diffs, totals = [], []
             for s in (2 * pair, 2 * pair + 1):
                 side_copy(step, s ^ 1).wait_recv()
-                mine = own[:, s * FS : (s + 1) * FS]
+                mine = sends[step, s]
                 other = recvs[step, s] * has[s]
-                other = jnp.concatenate([other, jnp.zeros((ROWS - SEND, FS), F32)], axis=0)
                 diffs.append(mine - other)
                 totals.append(mine + other if s % 2 == 1 else -(mine + other))
-            term = mix_terms(jnp.concatenate(diffs, axis=1), jnp.concatenate(totals, axis=1), full)
+            pad = jnp.zeros((ROWS - SEND, 2 * FS), F32)
+            difference = jnp.concatenate([jnp.concatenate(diffs, axis=1), pad], axis=0)
+            total = jnp.concatenate([jnp.concatenate(totals, axis=1), pad], axis=0)
+            term = mix_terms(difference, total, full)
             start = IF + pair * 2 * FS
             store_parts(term_b, term, 0, slice(start, start + 2 * FS), full)
 
@@ -357,18 +377,21 @@
 
     pairs = [(i, j) for i in range(ITERS + 1) for j in range(i, ITERS + 1)]
 
-    def products(c, accs):
+    def last_products(c, accs):
         accs = list(accs)
         base = pl.multiple_of(c * 8, 8)
         for b in range(NV):
             for lt in range(2):
                 lanes = slice(lt * 128, (lt + 1) * 128)
-                u = [us[k, b, pl.ds(base, 8), lanes] for k in range(ITERS + 1)]
-                for n, (i, j) in enumerate(pairs):
-                    accs[n] = accs[n] + u[i] * u[j]
+                v = us[ITERS, b, pl.ds(base, 8), lanes]
+                for k in range(ITERS):
+                    accs[k] = accs[k] + v * us[k, b, pl.ds(base, 8), lanes]
+                accs[ITERS] = accs[ITERS] + v * v
         return tuple(accs)
 
-    accs = lax.fori_loop(0, 16, products, tuple(jnp.zeros((8, 128), F32) for _ in pairs))
+    zero = jnp.zeros((8, 128), F32)
+    last = lax.fori_loop(0, 16, last_products, (zero,) * (ITERS + 1))
+    accs = [last[i] if j == ITERS else prods[early.index((i, j))] for i, j in pairs]
     rows = [jnp.sum(x, axis=0, keepdims=True) for x in accs]
     rows.append(jnp.zeros((1, 128), F32))
     x = jnp.concatenate(rows, axis=0)
@@ -377,7 +400,7 @@
     row = lax.broadcasted_iota(jnp.int32, (16, 128), 0)
     lane = lax.broadcasted_iota(jnp.int32, (16, 128), 1)
     x = jnp.sum(jnp.where((lane >= row * 8) & (lane < row * 8 + 8), x, 0.0), axis=0, keepdims=True)
-    gram[0] = jnp.broadcast_to(x, (8, 128))
+    gram[0] = x
 
     def sum_copy(k, i):
         return pltpu.make_async_remote_copy(
@@ -467,19 +490,19 @@
             pltpu.VMEM((NV, 384, E), F32),
             pltpu.VMEM((ROWS, COLS), F32),
             pltpu.VMEM((2 * ROWS, COLS), BF),
-            pltpu.VMEM((ROWS, 4 * FS), F32),
-            pltpu.VMEM((6 * ROWS, IF), BF),
+            pltpu.VMEM((6 * ROWS, E), BF),
             pltpu.VMEM((2 * ROWS, IF + 4 * FS), BF),
             pltpu.VMEM((ROWS, COLS), F32),
             pltpu.VMEM((NV, ROWS, E), F32),
             pltpu.VMEM((ITERS, 4, SEND, FS), F32),
             pltpu.VMEM((ITERS, 4, SEND, FS), F32),
-            pltpu.VMEM((len(STAGES), 8, 128), F32),
-            pltpu.VMEM((len(STAGES), 16, 8, 128), F32),
+            pltpu.VMEM((len(STAGES), 1, 128), F32),
+            pltpu.VMEM((len(STAGES), 16, 1, 128), F32),
             pltpu.SemaphoreType.DMA((ITERS, 4)),
             pltpu.SemaphoreType.DMA((ITERS, 4)),
             pltpu.SemaphoreType.DMA((len(STAGES), 16)),
             pltpu.SemaphoreType.DMA((len(STAGES), 16)),
+            pltpu.VMEM((ITERS * (ITERS + 1) // 2, 8, 128), F32),
         ],
         compiler_params=pltpu.CompilerParams(
             collective_id=0, has_side_effects=True, vmem_limit_bytes=44 * 1024 * 1024

time: 49.4 us -> 48.5 us (0.982)
  Pallas kernels: 48.4 us -> 47.3 us
    pallas_call x1, Pallas kernels: 48.4 us -> 47.3 us  [local(): pl.pallas_call(functools.partial(kernel, n_span, n_chord), out_shape=jax....]
where the time goes in v4:
time: 48.5 us; the launch traced here: 48.2 us
  Pallas kernels  47.3 us (98%)
  local copies, waits for them, and re-layouts  0.88 us (2%)
    pallas_call x1, Pallas kernels, local(): pl.pallas_call(functools.partial(kernel, n_span, n_chord), out_shape=jax....  47.3 us

profile of v4, /device:TPU:1, one launch (start us, length us, event | category | flops | bytes accessed | tf_op | source)
XLA Modules:
  0.0 48.2 jit_solution(15568289586035819876)
XLA Ops:
  0.0 47.3 %shard_map.136 = f32[6,125,256]{2,1,0:T(8,128)S(1)} custom-call(f32[6,125,256]{2,1,0:T(8,128)} %refs_0_.1, s32[256]{0:T(256)} %refs_1_.1, f32[256]{0:T(256)} %refs_2_.1, f32[3,6,6,256]{3,2,1,0:T(8,128)} %refs_3_.1, f32[6,6,256]{2,1,0:T(8,128)} %refs_4_.1, f32[6,6]{1,0:T(8,128)} %refs_5_.1, f32[6,6]{1,0:T(8,128)} %refs_6_.1, f32[512]{0:T(512)} %refs_7_.1, ...), custom_call_target="tpu_custom_call" | custom-call | tf_op jit(solution)/shard_map/pallas_call | solution.py:473
  47.3 0.9 %copy.16 = f32[6,125,256]{2,1,0:T(8,128)} copy(f32[6,125,256]{2,1,0:T(8,128)S(1)} %shard_map.136) | data formatting | bytes 1536000

commit v5 on v4

--- a/solution.py
+++ b/solution.py
@@ -368,8 +368,6 @@
             else:
                 t = dot(lift_mat[:, 0:ROWS], hi)
             us[step + 1, b] = (us[step + 1, b] + t) * active[...] - SHIFT * us[step, b]
-        for s in range(4):
-            side_copy(step, s).wait_send()
         return carry
 
     lax.fori_loop(0, FULL_STEPS, functools.partial(one_step, True), 0)
@@ -465,6 +463,9 @@
             out[b, :, lanes] = x
     for k, i in partners:
         sum_copy(k, i).wait_send()
+    for step in range(ITERS):
+        for s in range(4):
+            side_copy(step, s).wait_send()
 
 
 def local(n_span, n_chord, *args):

time: 48.5 us -> 48.5 us (level)
  no operation moved by 1% of the time
where the time goes in v5:
time: 48.5 us; the launch traced here: 48.3 us
  Pallas kernels  47.4 us (98%)
  local copies, waits for them, and re-layouts  0.88 us (2%)
    pallas_call x1, Pallas kernels, local(): pl.pallas_call(functools.partial(kernel, n_span, n_chord), out_shape=jax....  47.4 us

profile of v5, /device:TPU:1, one launch (start us, length us, event | category | flops | bytes accessed | tf_op | source)
XLA Modules:
  0.0 48.3 jit_solution(14617103165262487448)
XLA Ops:
  0.0 47.4 %shard_map.136 = f32[6,125,256]{2,1,0:T(8,128)S(1)} custom-call(f32[6,125,256]{2,1,0:T(8,128)} %refs_0_.1, s32[256]{0:T(256)} %refs_1_.1, f32[256]{0:T(256)} %refs_2_.1, f32[3,6,6,256]{3,2,1,0:T(8,128)} %refs_3_.1, f32[6,6,256]{2,1,0:T(8,128)} %refs_4_.1, f32[6,6]{1,0:T(8,128)} %refs_5_.1, f32[6,6]{1,0:T(8,128)} %refs_6_.1, f32[512]{0:T(512)} %refs_7_.1, ...), custom_call_target="tpu_custom_call" | custom-call | tf_op jit(solution)/shard_map/pallas_call | solution.py:474
  47.4 0.9 %copy.16 = f32[6,125,256]{2,1,0:T(8,128)} copy(f32[6,125,256]{2,1,0:T(8,128)S(1)} %shard_map.136) | data formatting | bytes 1536000
